TPU v7x, 32 devices: a whole 2x2x4 slice. The times are simulated.
32 devices in a mesh: row: 4 (over y, core), col: 8 (over z, x).
Axes of the slice: x: 2, y: 2, z: 4, core: 2. Of those that a mesh axis runs over, the one named last changes fastest.
Arguments:
- grad: bfloat16 [8192, 4096], P('row', 'col'), may hold values from -6 to 6
- basis_left: bfloat16 [8192, 8192], P('row', 'col'), may hold values from -0.0625 to 0.0625
- basis_right: bfloat16 [4096, 4096], P('row', 'col'), may hold values from -0.09375 to 0.09375
- first_moment: float32 [8192, 4096], P('col', 'row'), may hold values from -6 to 6
- second_moment: float32 [8192, 4096], P('col', 'row'), may hold values from 0.25 to 4
Outputs:
- update: bfloat16 [8192, 4096], P('row', 'col')
- first_new: float32 [8192, 4096], P('col', 'row')
- second_new: float32 [8192, 4096], P('col', 'row')
All inputs are finite; a program needn't handle non-finite values.
Results may differ from a plain program's by a relative error of at most 0.029.
Values may be sent and summed in bfloat16 or wider, within the bound.
No kernel may reach another device: no remote copies, remote signals or barrier semaphores. Data moves between devices by JAX's collectives and lax.ppermute only.
A program may use at most 128 MiB of HBM per device.

v0:
```python
import jax
import jax.numpy as jnp
from jax import lax
from jax.sharding import PartitionSpec as P


def rotate_forward(left_matrix, contract_dim, moving_matrix):

    def product(pieces, offset):
        return lax.dot_general(
            left_matrix,
            pieces,
            (((contract_dim,), (0,)), ((), ())),
            preferred_element_type=jnp.float32,
        )

    partial_terms = product(lax.all_gather(moving_matrix, "col", axis=1, tiled=True), jnp.int32(0))
    return lax.psum_scatter(
        partial_terms.astype(jnp.bfloat16), "row", scatter_dimension=1, tiled=True
    ).astype(jnp.float32)


def rotate_backward(left_matrix, moving_matrix):

    def product(pieces, offset):
        return lax.dot_general(
            left_matrix, pieces, (((1,), (1,)), ((), ())), preferred_element_type=jnp.float32
        )

    partial_terms = product(lax.all_gather(moving_matrix, "row", axis=0, tiled=True), jnp.int32(0))
    return lax.psum_scatter(
        partial_terms.astype(jnp.bfloat16), "col", scatter_dimension=1, tiled=True
    )


def per_device(grad, basis_left, basis_right, first_moment, second_moment):
    left_rotated = rotate_forward(basis_left, 0, grad).astype(jnp.bfloat16)
    rotated = rotate_forward(left_rotated, 1, basis_right)
    first_new = 0.9 * first_moment + 0.1 * rotated
    second_new = 0.95 * second_moment + 0.05 * rotated * rotated
    direction = (first_new / (jnp.sqrt(second_new) + 1e-08)).astype(jnp.bfloat16)
    back_left = rotate_backward(basis_left, direction.T)
    update = rotate_backward(back_left, basis_right)
    return (update, first_new, second_new)


def solution(mesh):
    in_specs = (P("row", "col"), P("row", "col"), P("row", "col"), P("col", "row"), P("col", "row"))
    out_specs = (P("row", "col"), P("col", "row"), P("col", "row"))
    return jax.shard_map(
        per_device, mesh=mesh, in_specs=in_specs, out_specs=out_specs, check_vma=False
    )
```

profile of v0, /device:TPU:0, one launch (start us, length us, event | category | flops | bytes accessed | tf_op | source)
XLA Modules:
  0.0 1217.0 jit_solution(10938397890762779576)
XLA Ops:
  7.2 0.0 all-gather.5.cloned.1.call-start
  7.2 0.7 all-gather.5.cloned.1.call-update
  7.9 0.0 all-gather.7.cloned.1.call-start
  7.9 0.7 all-gather.7.cloned.1.call-update
  8.6 0.0 reduce-scatter.5.cloned.1.call-start
  8.7 231.8 %all-gather.5.cloned.1.call-done = bf16[2048,4096]{1,0:T(8,128)(2,1)} async-done(((bf16[2048,512]{1,0:T(8,128)(2,1)}), bf16[2048,4096]{1,0:T(8,128)(2,1)}) %all-gather.5.cloned.1.call-update) | async-done | bytes 16777232 | tf_op jit(solution)/shard_map/all_gather | solution.py:17
  240.5 23.3 %convolution_convert_fusion.2 = bf16[1024,4096]{1,0:T(8,128)(2,1)} fusion(bf16[2048,1024]{1,0:T(8,128)(2,1)} %param.6, bf16[2048,4096]{1,0:T(8,128)(2,1)} %all-gather.5.cloned.1.call-done), kind=kOutput, calls=%fused_computation.3 | convolution fusion | flops 17184063488 | bytes 29360128 | tf_op jit(solution)/shard_map/dot_general | solution.py:10
  263.8 0.0 reduce-scatter.5.cloned.1.call-update
  263.9 0.0 reduce-scatter.7.cloned.1.call-start
  263.9 102.3 %all-gather.7.cloned.1.call-done = bf16[1024,4096]{1,0:T(8,128)(2,1)} async-done(((bf16[1024,512]{1,0:T(8,128)(2,1)}), bf16[1024,4096]{1,0:T(8,128)(2,1)}) %all-gather.7.cloned.1.call-update) | async-done | bytes 8388624 | tf_op jit(solution)/shard_map/all_gather | solution.py:17
  366.2 72.5 %reduce-scatter.5.cloned.1.call-done = bf16[1024,1024]{1,0:T(8,128)(2,1)} async-done(((bf16[1024,4096]{1,0:T(8,128)(2,1)}), bf16[1024,1024]{1,0:T(8,128)(2,1)}) %reduce-scatter.5.cloned.1.call-update) | async-done | bytes 2097168 | tf_op jit(solution)/shard_map/reduce_scatter | solution.py:18
  438.7 14.7 %convolution_convert_fusion.1 = bf16[1024,4096]{1,0:T(8,128)(2,1)} fusion(bf16[1024,1024]{1,0:T(8,128)(2,1)} %reduce-scatter.5.cloned.1.call-done, bf16[1024,4096]{1,0:T(8,128)(2,1)} %all-gather.7.cloned.1.call-done), kind=kOutput, calls=%fused_computation.2 | convolution fusion | flops 8594128896 | bytes 18874368 | tf_op jit(solution)/shard_map/dot_general | solution.py:10
  453.4 0.0 reduce-scatter.7.cloned.1.call-update
  453.4 0.0 all-gather.9.cloned.1.call-start
  453.5 71.8 %reduce-scatter.7.cloned.1.call-done = bf16[1024,1024]{1,0:T(8,128)(2,1)} async-done(((bf16[1024,4096]{1,0:T(8,128)(2,1)}), bf16[1024,1024]{1,0:T(8,128)(2,1)}) %reduce-scatter.7.cloned.1.call-update) | async-done | bytes 2097168 | tf_op jit(solution)/shard_map/reduce_scatter | solution.py:18
  525.3 7.3 fusion.2
  532.6 0.0 all-gather.9.cloned.1.call-update
  532.6 0.0 all-gather.11.cloned.1.call-start
  532.7 0.5 all-gather.11.cloned.1.call-update
  533.2 0.2 reduce-scatter.9.cloned.1.call-start
  533.4 57.7 %all-gather.9.cloned.1.call-done = bf16[4096,1024]{0,1:T(8,128)(2,1)} async-done(((bf16[1024,1024]{0,1:T(8,128)(2,1)}), bf16[4096,1024]{0,1:T(8,128)(2,1)}) %all-gather.9.cloned.1.call-update) | async-done | bytes 8388624 | tf_op jit(solution)/shard_map/all_gather | solution.py:30
  591.1 25.2 %convert_bitcast_fusion = bf16[2048,4096]{0,1:T(8,128)(2,1)} fusion(bf16[4096,1024]{0,1:T(8,128)(2,1)} %all-gather.9.cloned.1.call-done, bf16[2048,1024]{1,0:T(8,128)(2,1)} %param.6), kind=kOutput, calls=%fused_computation | convolution fusion | flops 17188257792 | bytes 29360128 | tf_op jit(solution)/shard_map/dot_general | solution.py:26
  616.3 0.0 reduce-scatter.9.cloned.1.call-update
  616.4 0.3 reduce-scatter.11.cloned.1.call-start
  616.6 10.4 all-gather.11.cloned.1.call-done
  627.0 286.4 %reduce-scatter.9.cloned.1.call-done = bf16[2048,512]{0,1:T(8,128)(2,1)} async-done(((bf16[2048,4096]{0,1:T(8,128)(2,1)}), bf16[2048,512]{0,1:T(8,128)(2,1)}) %reduce-scatter.9.cloned.1.call-update) | async-done | bytes 2097168 | tf_op jit(solution)/shard_map/reduce_scatter | solution.py:31
  913.4 14.9 %convolution_convert_fusion = bf16[2048,4096]{1,0:T(8,128)(2,1)} fusion(bf16[2048,512]{0,1:T(8,128)(2,1)} %reduce-scatter.9.cloned.1.call-done, bf16[4096,512]{1,0:T(8,128)(2,1)} %all-gather.11.cloned.1.call-done), kind=kOutput, calls=%fused_computation.1 | convolution fusion | flops 8598323200 | bytes 23068672 | tf_op jit(solution)/shard_map/dot_general | solution.py:26
  928.3 0.0 reduce-scatter.11.cloned.1.call-update
  928.3 281.9 %reduce-scatter.11.cloned.1.call-done = bf16[2048,512]{1,0:T(8,128)(2,1)} async-done(((bf16[2048,4096]{1,0:T(8,128)(2,1)}), bf16[2048,512]{1,0:T(8,128)(2,1)}) %reduce-scatter.11.cloned.1.call-update) | async-done | bytes 2097168 | tf_op jit(solution)/shard_map/reduce_scatter | solution.py:31
Async XLA Ops:
  7.2 233.4 %all-gather.5.cloned.1.call-start = ((), (), s32[]{:S(2)}) async-start(), calls=%async_computation.4 | async-start | bytes 18874368 | tf_op jit(solution)/shard_map/all_gather | solution.py:17
  7.9 358.3 %all-gather.7.cloned.1.call-start = ((), (), s32[]{:S(2)}) async-start(), calls=%async_computation.6 | async-start | bytes 9437184 | tf_op jit(solution)/shard_map/all_gather | solution.py:17
  8.6 430.0 %reduce-scatter.5.cloned.1.call-start = ((), (), s32[]{:S(2)}) async-start(), calls=%async_computation.5 | async-start | bytes 10485760 | tf_op jit(solution)/shard_map/reduce_scatter | solution.py:18
  263.9 261.4 %reduce-scatter.7.cloned.1.call-start = ((), (), s32[]{:S(2)}) async-start(), calls=%async_computation.7 | async-start | bytes 10485760 | tf_op jit(solution)/shard_map/reduce_scatter | solution.py:18
  453.4 137.7 %all-gather.9.cloned.1.call-start = ((), (), s32[]{:S(2)}) async-start(), calls=%async_computation.8 | async-start | bytes 10485760 | tf_op jit(solution)/shard_map/all_gather | solution.py:30
  532.6 94.4 %all-gather.11.cloned.1.call-start = ((), (), s32[]{:S(2)}) async-start(), calls=%async_computation.10 | async-start | bytes 5242880 | tf_op jit(solution)/shard_map/all_gather | solution.py:30
  533.2 380.2 %reduce-scatter.9.cloned.1.call-start = ((), (), s32[]{:S(2)}) async-start(), calls=%async_computation.9 | async-start | bytes 18874368 | tf_op jit(solution)/shard_map/reduce_scatter | solution.py:31
  616.4 593.8 %reduce-scatter.11.cloned.1.call-start = ((), (), s32[]{:S(2)}) async-start(), calls=%async_computation.11 | async-start | bytes 18874368 | tf_op jit(solution)/shard_map/reduce_scatter | solution.py:31
Sparse Core Ops, SparseCore 0:
  10.0 230.4 all-gather.4
  242.6 123.5 all-gather.6
  368.8 69.8 reduce-scatter.4
  453.6 71.6 reduce-scatter.6
  532.8 58.2 all-gather.8
  592.5 34.4 all-gather.10
  630.8 282.5 reduce-scatter.8
  928.5 281.7 reduce-scatter.10
where the time goes:
time: 1220 us
  waiting for transfers between devices  1120 us (92%)
  matrix products  78.2 us (6%)
  between operations  14.1 us (1%)
    reduce_scatter x2, waiting for transfers between devices, rotate_backward(): lax.psum_scatter(partial_terms.astype(jnp.bfloat16), 'col', scatter_dimen...  568 us
    all_gather x2, waiting for transfers between devices, rotate_forward(): lax.all_gather(moving_matrix, 'col', axis=1, tiled=True)  334 us
    reduce_scatter x2, waiting for transfers between devices, rotate_forward(): lax.psum_scatter(partial_terms.astype(jnp.bfloat16), 'row', scatter_dimen...  144 us
    all_gather x2, waiting for transfers between devices, rotate_backward(): lax.all_gather(moving_matrix, 'row', axis=0, tiled=True)  68 us
    dot_general x2, matrix products, product(): lax.dot_general(left_matrix, pieces, (((1,), (1,)), ((), ())), preferred_...  40.2 us
    dot_general x2, matrix products, product(): lax.dot_general(left_matrix, pieces, (((contract_dim,), (0,)), ((), ())),...  38 us
  transfers between devices with their start and end apart: 8, of which 8 were waited for; matrix products, arithmetic and copies ran while one was open for 4% of the time, Pallas kernels for 0%

commit v1 on v0

v1 whole, which is shorter than its diff:
```python
import jax
import jax.numpy as jnp
from jax import lax
from jax.sharding import PartitionSpec as P

BF16 = jnp.bfloat16
F32 = jnp.float32


def dot(a, b, contract):
    return lax.dot_general(a, b, ((contract[:1], contract[1:]), ((), ())), preferred_element_type=F32)


def solution(mesh):
    n_row, n_col = mesh.shape["row"], mesh.shape["col"]
    n_a = 4 if n_col % 4 == 0 else n_col
    n_b = n_col // n_a
    per_row = n_col // n_row

    def col_shift(x, da, db):
        perm = [
            (a * n_b + b, ((a + da) % n_a) * n_b + (b + db) % n_b)
            for a in range(n_a)
            for b in range(n_b)
        ]
        return lax.ppermute(x, "col", perm)

    def row_xor(x, k):
        return lax.ppermute(x, "row", [(r, r ^ k) for r in range(n_row)])

    def half_sum(theirs, mine_f32):
        got = row_xor(theirs.astype(BF16), 1)
        mine = (mine_f32 + got.astype(F32)).astype(BF16)
        k = 2
        while k < n_row:
            mine = (mine.astype(F32) + row_xor(mine, k).astype(F32)).astype(BF16)
            k *= 2
        return mine, row_xor(mine, 1)

    def per_device(grad, basis_left, basis_right, first_moment, second_moment):
        r = lax.axis_index("row")
        c = lax.axis_index("col")
        a, b = c // n_b, c % n_b
        core = r % 2
        width = grad.shape[1]
        half = width // 2
        sub = width // n_row
        own_i = basis_left.shape[1]

        lefts = [basis_left] + [col_shift(basis_left, 0, -k) for k in range(1, n_b)]
        left = jnp.concatenate(lefts, axis=1)

        g_theirs = lax.dynamic_slice_in_dim(grad, (1 - core) * half, half, 1)
        g_mine = lax.dynamic_slice_in_dim(grad, core * half, half, 1)
        pieces = []
        for s in range(n_a):
            if s:
                g_theirs, g_mine = col_shift(g_theirs, 1, 0), col_shift(g_mine, 1, 0)
            pieces += half_sum(dot(left, g_theirs, (0, 0)), dot(left, g_mine, (0, 0)))
        left_rotated = jnp.concatenate(pieces, axis=1)

        right_all = lax.all_gather(basis_right, "row", axis=0, tiled=True)
        right_all = lax.dynamic_slice_in_dim(right_all, r * sub, sub, 1)
        by_b = right_all.reshape(n_a, n_b, width, sub)

        def rows_of(which):
            return lax.dynamic_index_in_dim(by_b, which, 1, keepdims=False).reshape(n_a * width, sub)

        got = [rows_of(b)] + [col_shift(rows_of((b + k) % n_b), 0, k) for k in range(1, n_b)]
        stacked = jnp.stack(got, 0)
        right_s = jnp.concatenate(
            [lax.dynamic_index_in_dim(stacked, (b - q) % n_b, 0, keepdims=False) for q in range(n_b)], axis=1
        )

        def relative(x):
            parts = []
            for s in range(n_a):
                start = ((a - s) % n_a) * width
                parts.append(lax.dynamic_slice_in_dim(x, start + core * half, half, 0))
                parts.append(lax.dynamic_slice_in_dim(x, start + (1 - core) * half, half, 0))
            return jnp.concatenate(parts, axis=0)

        rights, rots = [], []
        for t in range(n_a):
            if t:
                right_s = col_shift(right_s, 1, 0)
            right_t = relative(right_s)
            rights.append(right_t)
            rot = dot(left_rotated[:own_i], right_t, (1, 0))
            for k in range(1, n_b):
                part = dot(left_rotated[k * own_i : (k + 1) * own_i], right_t, (1, 0))
                rot = rot + col_shift(part.astype(BF16), 0, k).astype(F32)
            rots.append(rot.astype(BF16))

        def in_order(parts):
            stacked = jnp.stack(parts, 0)
            return jnp.concatenate(
                [lax.dynamic_index_in_dim(stacked, (a - q) % n_a, 0, keepdims=False) for q in range(n_a)], axis=1
            )

        rot_cols = in_order(rots)
        right_cols = in_order(rights)
        piece = per_row * sub

        first_new, second_new = first_moment, second_moment
        directions, right_k = [], []
        for k in range(n_row):
            peer = r ^ k
            rot = lax.dynamic_slice_in_dim(rot_cols, peer * piece, piece, 1)
            right_k.append(lax.dynamic_slice_in_dim(right_cols, peer * piece, piece, 1))
            if k:
                rot = row_xor(rot, k)
            rot = rot.astype(F32)
            outs = []
            for q in range(per_row):
                start = (q * n_row + peer) * sub
                rot_q = rot[:, q * sub : (q + 1) * sub]
                first = 0.9 * lax.dynamic_slice_in_dim(first_moment, start, sub, 1) + 0.1 * rot_q
                second = 0.95 * lax.dynamic_slice_in_dim(second_moment, start, sub, 1) + 0.05 * rot_q * rot_q
                first_new = lax.dynamic_update_slice_in_dim(first_new, first, start, 1)
                second_new = lax.dynamic_update_slice_in_dim(second_new, second, start, 1)
                outs.append((first / (jnp.sqrt(second) + 1e-08)).astype(BF16))
            direction = jnp.concatenate(outs, axis=1)
            if k:
                direction = row_xor(direction, k)
            directions.append(direction)

        own = jnp.concatenate(directions, axis=1)
        rows = [own] + [
            jnp.concatenate([col_shift(d, 0, -k) for d in directions], axis=1) for k in range(1, n_b)
        ]
        direction = jnp.concatenate(rows, axis=0)
        right_k = jnp.concatenate(right_k, axis=1)

        u_mine = u_theirs = None
        for s in list(range(1, n_a)) + [0]:
            r_mine = right_k[s * width : s * width + half]
            r_theirs = right_k[s * width + half : (s + 1) * width]
            w_mine, w_theirs = half_sum(dot(direction, r_theirs, (1, 1)), dot(direction, r_mine, (1, 1)))
            new_mine, new_theirs = dot(left, w_mine, (1, 0)), dot(left, w_theirs, (1, 0))
            if u_mine is not None:
                new_mine = new_mine + col_shift(u_mine, 1, 0).astype(F32)
                new_theirs = new_theirs + col_shift(u_theirs, 1, 0).astype(F32)
            u_mine, u_theirs = new_mine.astype(BF16), new_theirs.astype(BF16)
        update = jnp.where(
            core == 0,
            jnp.concatenate([u_mine, u_theirs], axis=1),
            jnp.concatenate([u_theirs, u_mine], axis=1),
        )
        return update, first_new, second_new

    in_specs = (P("row", "col"), P("row", "col"), P("row", "col"), P("col", "row"), P("col", "row"))
    out_specs = (P("row", "col"), P("col", "row"), P("col", "row"))
    return jax.shard_map(per_device, mesh=mesh, in_specs=in_specs, out_specs=out_specs, check_vma=False)
```

time: 1220 us -> 693 us (0.57)
  waiting for transfers between devices: 1120 us -> 505 us
  starting transfers between devices: 0.72 us -> 31.8 us
  local copies, waits for them, and re-layouts: 0 us -> 23.7 us
  other arithmetic: 7.3 us -> 30.4 us
    reduce_scatter x4 -> x0, waiting for transfers between devices: 713 us -> none  [the longest x2 568 us: rotate_backward(): lax.psum_scatter(partial_terms.astype(jnp.bfloat16), 'col', scatter_dimen...]
    ppermute x0 -> x55, waiting for transfers between devices: none -> 505 us  [the longest x25 351 us: col_shift(): return lax.ppermute(x, 'col', perm)]
    all_gather x4 -> x1, waiting for transfers between devices: 402 us -> 0.01 us  [per_device(): right_all = lax.all_gather(basis_right, 'row', axis=0, tiled=True)]
    ppermute x0 -> x55, starting transfers between devices: none -> 31.8 us  [the longest x30 16.8 us: row_xor(): return lax.ppermute(x, 'row', [(r, r ^ k) for r in range(n_row)])]
    concatenate x0 -> x10, other arithmetic: none -> 15 us  [the longest x1 11.2 us: per_device(): direction = jnp.concatenate(rows, axis=0)]
    dynamic_slice x0 -> x9, local copies, waits for them, and re-layouts: none -> 14.4 us  [the longest x5 9.63 us: in_order(): lax.dynamic_index_in_dim(stacked, (a - q) % n_a, 0, keepdims=False)]
    dot_general x4 -> x32, matrix products: 78.2 us -> 76 us  [dot(): lax.dot_general(a, b, ((contract[:1], contract[1:]), ((), ())), preferred...]
  transfers between devices with their start and end apart: 8 -> 56, of which waited for: 8 -> 31; matrix products, arithmetic and copies ran while one was open for 4% -> 13% of each run, Pallas kernels for 0% -> 0%
where the time goes in v1:
time: 693 us; the launch traced here: 683 us
  waiting for transfers between devices  505 us (73%)
  matrix products  76 us (11%)
  starting transfers between devices  31.8 us (5%)
  other arithmetic  30.4 us (4%)
  local copies, waits for them, and re-layouts  23.7 us (3%)
  between operations  15.9 us (2%)
    ppermute x25, waiting for transfers between devices, col_shift(): return lax.ppermute(x, 'col', perm)  351 us
    ppermute x30, waiting for transfers between devices, row_xor(): return lax.ppermute(x, 'row', [(r, r ^ k) for r in range(n_row)])  154 us
    dot_general x32, matrix products, dot(): lax.dot_general(a, b, ((contract[:1], contract[1:]), ((), ())), preferred...  76 us
    ppermute x30, starting transfers between devices, row_xor(): return lax.ppermute(x, 'row', [(r, r ^ k) for r in range(n_row)])  16.8 us
    ppermute x25, starting transfers between devices, col_shift(): return lax.ppermute(x, 'col', perm)  14.9 us
  transfers between devices with their start and end apart: 56, of which 31 were waited for; matrix products, arithmetic and copies ran while one was open for 13% of the time, Pallas kernels for 0%

profile of v1, /device:TPU:0, one launch (start us, length us, event | category | flops | bytes accessed | tf_op | source)
XLA Modules:
  0.0 682.7 jit_solution(15013119387810922747)
XLA Ops:
  7.2 3.0 collective-permute-start
  10.2 1.7 constant_dynamic-slice_fusion.14
  11.9 1.6 collective-permute-start.4
  15.1 24.7 %collective-permute-done.4 = bf16[2048,256]{1,0:T(8,128)(2,1)S(1)} collective-permute-done((bf16[2048,256]{1,0:T(8,128)(2,1)S(1)}, bf16[2048,256]{1,0:T(8,128)(2,1)S(1)}, u32[]{:S(2)}, u32[]{:S(2)}) %collective-permute-start.4) | collective-permute-done | bytes 1048608 | tf_op jit(solution)/shard_map/ppermute | solution.py:26
  39.8 22.6 %collective-permute-done.5 = bf16[2048,256]{1,0:T(8,128)(2,1)} collective-permute-done((bf16[2048,256]{1,0:T(8,128)(2,1)S(1)}, bf16[2048,256]{1,0:T(8,128)(2,1)}, u32[]{:S(2)}, u32[]{:S(2)}) %collective-permute-start.5) | collective-permute-done | bytes 1048608 | tf_op jit(solution)/shard_map/ppermute | solution.py:26
  62.7 2.6 constant_dynamic-update-slice_fusion.1
  65.4 19.5 %collective-permute-done.9 = bf16[2048,256]{1,0:T(8,128)(2,1)} collective-permute-done((bf16[2048,256]{1,0:T(8,128)(2,1)S(1)}, bf16[2048,256]{1,0:T(8,128)(2,1)}, u32[]{:S(2)}, u32[]{:S(2)}) %collective-permute-start.9) | collective-permute-done | bytes 1048608 | tf_op jit(solution)/shard_map/ppermute | solution.py:26
  84.9 22.5 %collective-permute-done.10 = bf16[2048,256]{1,0:T(8,128)(2,1)} collective-permute-done((bf16[2048,256]{1,0:T(8,128)(2,1)}, bf16[2048,256]{1,0:T(8,128)(2,1)}, u32[]{:S(2)}, u32[]{:S(2)}) %collective-permute-start.10) | collective-permute-done | bytes 1048608 | tf_op jit(solution)/shard_map/ppermute | solution.py:26
  107.3 2.6 constant_dynamic-update-slice_fusion
  110.0 2.4 convolution_convert_fusion.9
  112.5 3.9 convolution_convert_fusion.8
  116.7 3.6 convolution_convert_fusion.7
  120.7 30.1 %collective-permute-done.15 = bf16[2048,256]{1,0:T(8,128)(2,1)S(1)} collective-permute-done((bf16[2048,256]{1,0:T(8,128)(2,1)}, bf16[2048,256]{1,0:T(8,128)(2,1)S(1)}, u32[]{:S(2)}, u32[]{:S(2)}) %collective-permute-start.15) | collective-permute-done | bytes 1048608 | tf_op jit(solution)/shard_map/ppermute | solution.py:26
  150.8 3.4 convolution_convert_fusion.6
  154.2 3.4 fusion.16
  159.1 2.8 fusion.17
  162.5 3.7 fusion.18
  169.3 14.6 %collective-permute-done.2 = bf16[2048,256]{0,1:T(8,128)(2,1)} collective-permute-done((bf16[2048,256]{0,1:T(8,128)(2,1)}, bf16[2048,256]{0,1:T(8,128)(2,1)}, u32[]{:S(2)}, u32[]{:S(2)}) %collective-permute-start.2) | collective-permute-done | bytes 1048608 | tf_op jit(solution)/shard_map/ppermute | solution.py:29
  184.4 2.0 constant_dynamic-update-slice_fusion.9
  186.5 3.9 fusion.19
  190.5 1.6 collective-permute-start.17
  192.1 5.0 collective-permute-done.19
  197.8 8.5 %collective-permute-done.7 = bf16[2048,256]{0,1:T(8,128)(2,1)} collective-permute-done((bf16[2048,256]{0,1:T(8,128)(2,1)S(1)}, bf16[2048,256]{0,1:T(8,128)(2,1)}, u32[]{:S(2)}, u32[]{:S(2)}) %collective-permute-start.7) | collective-permute-done | bytes 1048608 | tf_op jit(solution)/shard_map/ppermute | solution.py:29
  206.3 1.7 constant_dynamic-update-slice_fusion.7
  208.2 14.7 %collective-permute-done.21 = bf16[2048,256]{1,0:T(8,128)(2,1)S(1)} collective-permute-done((bf16[2048,256]{1,0:T(8,128)(2,1)S(1)}, bf16[2048,256]{1,0:T(8,128)(2,1)S(1)}, u32[]{:S(2)}, u32[]{:S(2)}) %collective-permute-start.21) | collective-permute-done | bytes 1048608 | tf_op jit(solution)/shard_map/ppermute | solution.py:26
  223.2 5.5 collective-permute-done.12
  229.2 18.2 %collective-permute-done.23 = bf16[2048,256]{1,0:T(8,128)(2,1)S(1)} collective-permute-done((bf16[2048,256]{1,0:T(8,128)(2,1)S(1)}, bf16[2048,256]{1,0:T(8,128)(2,1)S(1)}, u32[]{:S(2)}, u32[]{:S(2)}) %collective-permute-start.23) | collective-permute-done | bytes 1048608 | tf_op jit(solution)/shard_map/ppermute | solution.py:26
  247.7 3.1 collective-permute-done.17
  251.3 19.6 %collective-permute-done.25 = bf16[2048,256]{1,0:T(8,128)(2,1)S(1)} collective-permute-done((bf16[2048,256]{1,0:T(8,128)(2,1)S(1)}, bf16[2048,256]{1,0:T(8,128)(2,1)S(1)}, u32[]{:S(2)}, u32[]{:S(2)}) %collective-permute-start.25) | collective-permute-done | bytes 1048608 | tf_op jit(solution)/shard_map/ppermute | solution.py:26
  283.9 8.1 %collective-permute-done.26 = bf16[1024,256]{0,1:T(8,128)(2,1)S(1)} collective-permute-done((bf16[1024,256]{0,1:T(8,128)(2,1)S(1)}, bf16[1024,256]{0,1:T(8,128)(2,1)S(1)}, u32[]{:S(2)}, u32[]{:S(2)}) %collective-permute-start.26) | collective-permute-done | bytes 524320 | tf_op jit(solution)/shard_map/ppermute | solution.py:26
  293.3 9.9 %collective-permute-done.24 = bf16[1024,256]{0,1:T(8,128)(2,1)S(1)} collective-permute-done((bf16[1024,256]{0,1:T(8,128)(2,1)S(1)}, bf16[1024,256]{0,1:T(8,128)(2,1)S(1)}, u32[]{:S(2)}, u32[]{:S(2)}) %collective-permute-start.24) | collective-permute-done | bytes 524320 | tf_op jit(solution)/shard_map/ppermute | solution.py:26
  304.5 9.9 %collective-permute-done.22 = bf16[1024,256]{0,1:T(8,128)(2,1)S(1)} collective-permute-done((bf16[1024,256]{0,1:T(8,128)(2,1)S(1)}, bf16[1024,256]{0,1:T(8,128)(2,1)S(1)}, u32[]{:S(2)}, u32[]{:S(2)}) %collective-permute-start.22) | collective-permute-done | bytes 524320 | tf_op jit(solution)/shard_map/ppermute | solution.py:26
  315.7 4.7 collective-permute-done.20
  323.3 2.0 copy.34
  325.4 2.0 copy.33
  327.4 2.1 copy.32
  329.5 2.1 copy.31
  331.6 2.0 pad_maximum_fusion.5
  334.4 1.7 collective-permute-start.31
  336.7 1.8 fusion.128
  339.4 20.5 %collective-permute-done.29 = bf16[1024,256]{1,0:T(8,128)(2,1)S(1)} collective-permute-done((bf16[1024,256]{1,0:T(8,128)(2,1)S(1)}, bf16[1024,256]{1,0:T(8,128)(2,1)S(1)}, u32[]{:S(2)}, u32[]{:S(2)}) %collective-permute-start.29) | collective-permute-done | bytes 524320 | tf_op jit(solution)/shard_map/ppermute | solution.py:29
  361.1 2.0 divide_convert_fusion.5
  367.1 10.3 %collective-permute-done.32 = bf16[1024,256]{1,0:T(8,128)(2,1)S(1)} collective-permute-done((bf16[1024,256]{1,0:T(8,128)(2,1)S(1)}, bf16[1024,256]{1,0:T(8,128)(2,1)S(1)}, u32[]{:S(2)}, u32[]{:S(2)}) %collective-permute-start.32) | collective-permute-done | bytes 524320 | tf_op jit(solution)/shard_map/ppermute | solution.py:29
  378.1 10.7 %collective-permute-done.30 = bf16[1024,256]{1,0:T(8,128)(2,1)S(1)} collective-permute-done((bf16[1024,256]{1,0:T(8,128)(2,1)S(1)}, bf16[1024,256]{1,0:T(8,128)(2,1)S(1)}, u32[]{:S(2)}, u32[]{:S(2)}) %collective-permute-start.30) | collective-permute-done | bytes 524320 | tf_op jit(solution)/shard_map/ppermute | solution.py:29
  391.7 11.8 %collective-permute-done.35 = bf16[1024,256]{1,0:T(8,128)(2,1)S(1)} collective-permute-done((bf16[1024,256]{1,0:T(8,128)(2,1)S(1)}, bf16[1024,256]{1,0:T(8,128)(2,1)S(1)}, u32[]{:S(2)}, u32[]{:S(2)}) %collective-permute-start.35) | collective-permute-done | bytes 524320 | tf_op jit(solution)/shard_map/ppermute | solution.py:26
  403.6 10.5 %collective-permute-done.34 = bf16[1024,256]{1,0:T(8,128)(2,1)S(1)} collective-permute-done((bf16[1024,256]{1,0:T(8,128)(2,1)S(1)}, bf16[1024,256]{1,0:T(8,128)(2,1)S(1)}, u32[]{:S(2)}, u32[]{:S(2)}) %collective-permute-start.34) | collective-permute-done | bytes 524320 | tf_op jit(solution)/shard_map/ppermute | solution.py:26
  414.1 11.2 %maximum_maximum_fusion = bf16[2048,1024]{1,0:T(8,128)(2,1)S(1)} fusion(bf16[1024,256]{1,0:T(8,128)(2,1)S(1)} %collective-permute-done.36, bf16[1024,256]{1,0:T(8,128)(2,1)S(1)} %collective-permute-done.35, bf16[1024,256]{1,0:T(8,128)(2,1)S(1)} %collective-permute-done.34, bf16[1024,256]{1,0:T(8,128)(2,1)S(1)} %collective-permute-done.33, ...), kind=kLoop, calls=%fused_computation | loop fusion | flops 20971520 | bytes 8388608 | tf_op jit(solution)/shard_map/concatenate | solution.py:132
  441.6 17.6 %collective-permute-done.44 = bf16[2048,256]{1,0:T(8,128)(2,1)S(1)} collective-permute-done((bf16[2048,256]{1,0:T(8,128)(2,1)S(1)}, bf16[2048,256]{1,0:T(8,128)(2,1)S(1)}, u32[]{:S(2)}, u32[]{:S(2)}) %collective-permute-start.44) | collective-permute-done | bytes 1048608 | tf_op jit(solution)/shard_map/ppermute | solution.py:29
  459.6 2.7 convolution_convert_fusion.5
  462.3 63.4 %collective-permute-done.42 = bf16[2048,256]{1,0:T(8,128)(2,1)S(1)} collective-permute-done((bf16[2048,256]{1,0:T(8,128)(2,1)S(1)}, bf16[2048,256]{1,0:T(8,128)(2,1)S(1)}, u32[]{:S(2)}, u32[]{:S(2)}) %collective-permute-start.42) | collective-permute-done | bytes 1048608 | tf_op jit(solution)/shard_map/ppermute | solution.py:29
  526.2 2.4 convolution_convert_fusion.4
  529.4 24.4 %collective-permute-done.45 = bf16[2048,256]{0,1:T(8,128)(2,1)S(1)} collective-permute-done((bf16[2048,256]{0,1:T(8,128)(2,1)S(1)}, bf16[2048,256]{0,1:T(8,128)(2,1)S(1)}, u32[]{:S(2)}, u32[]{:S(2)}) %collective-permute-start.45) | collective-permute-done | bytes 1048608 | tf_op jit(solution)/shard_map/ppermute | solution.py:26
  553.9 2.4 fusion.22
  556.4 20.0 %collective-permute-done.52 = bf16[2048,256]{0,1:T(8,128)(2,1)S(1)} collective-permute-done((bf16[2048,256]{0,1:T(8,128)(2,1)S(1)}, bf16[2048,256]{0,1:T(8,128)(2,1)S(1)}, u32[]{:S(2)}, u32[]{:S(2)}) %collective-permute-start.52) | collective-permute-done | bytes 1048608 | tf_op jit(solution)/shard_map/ppermute | solution.py:26
  576.4 2.4 fusion.25
  579.2 19.6 %collective-permute-done.46 = bf16[2048,256]{0,1:T(8,128)(2,1)S(1)} collective-permute-done((bf16[2048,256]{0,1:T(8,128)(2,1)S(1)}, bf16[2048,256]{0,1:T(8,128)(2,1)S(1)}, u32[]{:S(2)}, u32[]{:S(2)}) %collective-permute-start.46) | collective-permute-done | bytes 1048608 | tf_op jit(solution)/shard_map/ppermute | solution.py:26
  598.8 2.4 fusion.21
  601.6 19.7 %collective-permute-done.53 = bf16[2048,256]{0,1:T(8,128)(2,1)S(1)} collective-permute-done((bf16[2048,256]{0,1:T(8,128)(2,1)S(1)}, bf16[2048,256]{0,1:T(8,128)(2,1)S(1)}, u32[]{:S(2)}, u32[]{:S(2)}) %collective-permute-start.53) | collective-permute-done | bytes 1048608 | tf_op jit(solution)/shard_map/ppermute | solution.py:26
  621.3 3.4 fusion.24
  624.7 19.2 %collective-permute-done.47 = bf16[2048,256]{0,1:T(8,128)(2,1)} collective-permute-done((bf16[2048,256]{0,1:T(8,128)(2,1)S(1)}, bf16[2048,256]{0,1:T(8,128)(2,1)}, u32[]{:S(2)}, u32[]{:S(2)}) %collective-permute-start.47) | collective-permute-done | bytes 1048608 | tf_op jit(solution)/shard_map/ppermute | solution.py:26
  643.9 6.1 fusion.20
  650.0 15.9 %collective-permute-done.54 = bf16[2048,256]{0,1:T(8,128)(2,1)} collective-permute-done((bf16[2048,256]{0,1:T(8,128)(2,1)}, bf16[2048,256]{0,1:T(8,128)(2,1)}, u32[]{:S(2)}, u32[]{:S(2)}) %collective-permute-start.54) | collective-permute-done | bytes 1048608 | tf_op jit(solution)/shard_map/ppermute | solution.py:26
  665.9 6.1 fusion.23
  672.9 2.5 copy.41
  (198 shorter events, 60.8 us)
Async XLA Ops:
  7.2 160.6 %all-gather.2.cloned.1.call-start = ((), (), s32[]{:S(2)}) async-start(), calls=%async_computation | async-start | bytes 5242880 | tf_op jit(solution)/shard_map/all_gather | solution.py:62
  7.2 100.1 %collective-permute-start = (bf16[2048,1024]{1,0:T(8,128)(2,1)}, bf16[2048,1024]{1,0:T(8,128)(2,1)}, u32[]{:S(2)}, u32[]{:S(2)}) collective-permute-start(bf16[2048,1024]{1,0:T(8,128)(2,1)} %param.6), channel_id=1, source_target_pairs={{0,1},{1,0},{2,3},{3,2},{4,5},{5,4},{6,7},{7,6},{8,9},{9,8},{10,11... | collective-permute-start | bytes 12582920 | tf_op jit(solution)/shard_map/ppermute | solution.py:26
  11.9 27.9 %collective-permute-start.4 = (bf16[2048,256]{1,0:T(8,128)(2,1)S(1)}, bf16[2048,256]{1,0:T(8,128)(2,1)S(1)}, u32[]{:S(2)}, u32[]{:S(2)}) collective-permute-start(bf16[2048,256]{1,0:T(8,128)(2,1)S(1)} %get-tuple-element.50), channel_id=1, source_target_pairs={{0,2},{1,3},{2,4},{3,5},{4,6},{5,7},{6,0},{7,1},{8,10},{9,11},{10,... | collective-permute-start | bytes 3145736 | tf_op jit(solution)/shard_map/ppermute | solution.py:26
  13.5 48.9 %collective-permute-start.5 = (bf16[2048,256]{1,0:T(8,128)(2,1)S(1)}, bf16[2048,256]{1,0:T(8,128)(2,1)}, u32[]{:S(2)}, u32[]{:S(2)}) collective-permute-start(bf16[2048,256]{1,0:T(8,128)(2,1)S(1)} %get-tuple-element.49), channel_id=1, source_target_pairs={{0,2},{1,3},{2,4},{3,5},{4,6},{5,7},{6,0},{7,1},{8,10},{9,11},{10,... | collective-permute-start | bytes 3145736 | tf_op jit(solution)/shard_map/ppermute | solution.py:26
  39.8 22.8 %copy-start.9 = (bf16[2048,256]{1,0:T(8,128)(2,1)}, bf16[2048,256]{1,0:T(8,128)(2,1)S(1)}, u32[]{:S(2)}) copy-start(bf16[2048,256]{1,0:T(8,128)(2,1)S(1)} %collective-permute-done.4) | copy-start | bytes 3145732
  39.8 45.0 %collective-permute-start.9 = (bf16[2048,256]{1,0:T(8,128)(2,1)S(1)}, bf16[2048,256]{1,0:T(8,128)(2,1)}, u32[]{:S(2)}, u32[]{:S(2)}) collective-permute-start(bf16[2048,256]{1,0:T(8,128)(2,1)S(1)} %collective-permute-done.4), channel_id=1, source_target_pairs={{0,2},{1,3},{2,4},{3,5},{4,6},{5,7},{6,0},{7,1},{8,10},{9,11},{10,... | collective-permute-start | bytes 3145736 | tf_op jit(solution)/shard_map/ppermute | solution.py:26
  62.4 44.9 %collective-permute-start.10 = (bf16[2048,256]{1,0:T(8,128)(2,1)}, bf16[2048,256]{1,0:T(8,128)(2,1)}, u32[]{:S(2)}, u32[]{:S(2)}) collective-permute-start(bf16[2048,256]{1,0:T(8,128)(2,1)} %collective-permute-done.5), channel_id=1, source_target_pairs={{0,2},{1,3},{2,4},{3,5},{4,6},{5,7},{6,0},{7,1},{8,10},{9,11},{10,... | collective-permute-start | bytes 3145736 | tf_op jit(solution)/shard_map/ppermute | solution.py:26
  84.9 101.6 %collective-permute-start.14 = (bf16[2048,256]{1,0:T(8,128)(2,1)}, bf16[2048,256]{1,0:T(8,128)(2,1)}, u32[]{:S(2)}, u32[]{:S(2)}) collective-permute-start(bf16[2048,256]{1,0:T(8,128)(2,1)} %collective-permute-done.9), channel_id=1, source_target_pairs={{0,2},{1,3},{2,4},{3,5},{4,6},{5,7},{6,0},{7,1},{8,10},{9,11},{10,... | collective-permute-start | bytes 3145736 | tf_op jit(solution)/shard_map/ppermute | solution.py:26
  107.3 43.4 %collective-permute-start.15 = (bf16[2048,256]{1,0:T(8,128)(2,1)}, bf16[2048,256]{1,0:T(8,128)(2,1)S(1)}, u32[]{:S(2)}, u32[]{:S(2)}) collective-permute-start(bf16[2048,256]{1,0:T(8,128)(2,1)} %collective-permute-done.10), channel_id=1, source_target_pairs={{0,2},{1,3},{2,4},{3,5},{4,6},{5,7},{6,0},{7,1},{8,10},{9,11},{10,... | collective-permute-start | bytes 3145736 | tf_op jit(solution)/shard_map/ppermute | solution.py:26
  110.0 52.5 %copy-start.7 = (bf16[2048,2048]{1,0:T(8,128)(2,1)}, bf16[2048,2048]{1,0:T(8,128)(2,1)S(1)}, u32[]{:S(2)}) copy-start(bf16[2048,2048]{1,0:T(8,128)(2,1)S(1)} %constant_dynamic-update-slice_fusion) | copy-start | bytes 25165828
  112.4 41.8 %collective-permute-start.1 = (bf16[2048,256]{0,1:T(8,128)(2,1)S(1)}, bf16[2048,256]{0,1:T(8,128)(2,1)S(1)}, u32[]{:S(2)}, u32[]{:S(2)}) collective-permute-start(bf16[2048,256]{0,1:T(8,128)(2,1)S(1)} %convolution_convert_fusion.9), channel_id=1, source_target_pairs={{0,8},{8,0},{16,24},{24,16},{1,9},{9,1},{17,25},{25,17},{2,10},{10... | collective-permute-start | bytes 3145736 | tf_op jit(solution)/shard_map/ppermute | solution.py:29
  116.4 42.7 %collective-permute-start.6 = (bf16[2048,256]{0,1:T(8,128)(2,1)S(1)}, bf16[2048,256]{0,1:T(8,128)(2,1)S(1)}, u32[]{:S(2)}, u32[]{:S(2)}) collective-permute-start(bf16[2048,256]{0,1:T(8,128)(2,1)S(1)} %convolution_convert_fusion.8), channel_id=1, source_target_pairs={{0,8},{8,0},{16,24},{24,16},{1,9},{9,1},{17,25},{25,17},{2,10},{10... | collective-permute-start | bytes 3145736 | tf_op jit(solution)/shard_map/ppermute | solution.py:29
  120.3 42.1 %collective-permute-start.11 = (bf16[2048,256]{0,1:T(8,128)(2,1)S(1)}, bf16[2048,256]{0,1:T(8,128)(2,1)S(1)}, u32[]{:S(2)}, u32[]{:S(2)}) collective-permute-start(bf16[2048,256]{0,1:T(8,128)(2,1)S(1)} %convolution_convert_fusion.7), channel_id=1, source_target_pairs={{0,8},{8,0},{16,24},{24,16},{1,9},{9,1},{17,25},{25,17},{2,10},{10... | collective-permute-start | bytes 3145736 | tf_op jit(solution)/shard_map/ppermute | solution.py:29
  154.2 32.4 %collective-permute-start.16 = (bf16[2048,256]{0,1:T(8,128)(2,1)}, bf16[2048,256]{0,1:T(8,128)(2,1)}, u32[]{:S(2)}, u32[]{:S(2)}) collective-permute-start(bf16[2048,256]{0,1:T(8,128)(2,1)} %convolution_convert_fusion.6), channel_id=1, source_target_pairs={{0,8},{8,0},{16,24},{24,16},{1,9},{9,1},{17,25},{25,17},{2,10},{10... | collective-permute-start | bytes 3145736 | tf_op jit(solution)/shard_map/ppermute | solution.py:29
  157.6 26.3 %collective-permute-start.2 = (bf16[2048,256]{0,1:T(8,128)(2,1)}, bf16[2048,256]{0,1:T(8,128)(2,1)}, u32[]{:S(2)}, u32[]{:S(2)}) collective-permute-start(bf16[2048,256]{0,1:T(8,128)(2,1)} %fusion.16), channel_id=1, source_target_pairs={{0,16},{8,24},{16,0},{24,8},{1,17},{9,25},{17,1},{25,9},{2,18},{10... | collective-permute-start | bytes 3145736 | tf_op jit(solution)/shard_map/ppermute | solution.py:29
  161.9 44.4 %collective-permute-start.7 = (bf16[2048,256]{0,1:T(8,128)(2,1)S(1)}, bf16[2048,256]{0,1:T(8,128)(2,1)}, u32[]{:S(2)}, u32[]{:S(2)}) collective-permute-start(bf16[2048,256]{0,1:T(8,128)(2,1)S(1)} %fusion.17), channel_id=1, source_target_pairs={{0,16},{8,24},{16,0},{24,8},{1,17},{9,25},{17,1},{25,9},{2,18},{10... | collective-permute-start | bytes 3145736 | tf_op jit(solution)/shard_map/ppermute | solution.py:29
  166.1 62.5 %collective-permute-start.12 = (bf16[2048,256]{0,1:T(8,128)(2,1)S(1)}, bf16[2048,256]{0,1:T(8,128)(2,1)S(1)}, u32[]{:S(2)}, u32[]{:S(2)}) collective-permute-start(bf16[2048,256]{0,1:T(8,128)(2,1)S(1)} %fusion.18), channel_id=1, source_target_pairs={{0,16},{8,24},{16,0},{24,8},{1,17},{9,25},{17,1},{25,9},{2,18},{10... | collective-permute-start | bytes 3145736 | tf_op jit(solution)/shard_map/ppermute | solution.py:29
  167.7 18.8 %copy-start.8 = (bf16[2048,2048]{1,0:T(8,128)(2,1)S(1)}, bf16[2048,2048]{1,0:T(8,128)(2,1)}, u32[]{:S(2)}) copy-start(bf16[2048,2048]{1,0:T(8,128)(2,1)} %copy-done.7) | copy-start | bytes 25165828
  183.8 13.2 %collective-permute-start.19 = (bf16[2048,128]{1,0:T(8,128)(2,1)S(1)}, bf16[2048,128]{1,0:T(8,128)(2,1)S(1)}, u32[]{:S(2)}, u32[]{:S(2)}) collective-permute-start(bf16[2048,128]{1,0:T(8,128)(2,1)S(1)} %bitcast.92), channel_id=1, source_target_pairs={{0,1},{1,0},{2,3},{3,2},{4,5},{5,4},{6,7},{7,6},{8,9},{9,8},{10,11... | collective-permute-start | bytes 1572872 | tf_op jit(solution)/shard_map/ppermute | solution.py:26
  186.4 11.3 %collective-permute-start.3 = (bf16[2048,256]{0,1:T(8,128)(2,1)S(1)}, bf16[2048,256]{0,1:T(8,128)(2,1)S(1)}, u32[]{:S(2)}, u32[]{:S(2)}) collective-permute-start(bf16[2048,256]{0,1:T(8,128)(2,1)S(1)} %get-tuple-element.20), channel_id=1, source_target_pairs={{0,8},{8,0},{16,24},{24,16},{1,9},{9,1},{17,25},{25,17},{2,10},{10... | collective-permute-start | bytes 3145736 | tf_op jit(solution)/shard_map/ppermute | solution.py:29
  190.5 60.3 %collective-permute-start.17 = (bf16[2048,256]{0,1:T(8,128)(2,1)S(1)}, bf16[2048,256]{0,1:T(8,128)(2,1)S(1)}, u32[]{:S(2)}, u32[]{:S(2)}) collective-permute-start(bf16[2048,256]{0,1:T(8,128)(2,1)S(1)} %fusion.19), channel_id=1, source_target_pairs={{0,16},{8,24},{16,0},{24,8},{1,17},{9,25},{17,1},{25,9},{2,18},{10... | collective-permute-start | bytes 3145736 | tf_op jit(solution)/shard_map/ppermute | solution.py:29
  197.5 25.4 %collective-permute-start.21 = (bf16[2048,256]{1,0:T(8,128)(2,1)S(1)}, bf16[2048,256]{1,0:T(8,128)(2,1)S(1)}, u32[]{:S(2)}, u32[]{:S(2)}) collective-permute-start(bf16[2048,256]{1,0:T(8,128)(2,1)S(1)} %pad_maximum_fusion.3), channel_id=1, source_target_pairs={{0,2},{1,3},{2,4},{3,5},{4,6},{5,7},{6,0},{7,1},{8,10},{9,11},{10,... | collective-permute-start | bytes 3145736 | tf_op jit(solution)/shard_map/ppermute | solution.py:26
  208.0 15.1 %collective-permute-start.8 = (bf16[2048,256]{0,1:T(8,128)(2,1)S(1)}, bf16[2048,256]{0,1:T(8,128)(2,1)S(1)}, u32[]{:S(2)}, u32[]{:S(2)}) collective-permute-start(bf16[2048,256]{0,1:T(8,128)(2,1)S(1)} %get-tuple-element.18), channel_id=1, source_target_pairs={{0,8},{8,0},{16,24},{24,16},{1,9},{9,1},{17,25},{25,17},{2,10},{10... | collective-permute-start | bytes 3145736 | tf_op jit(solution)/shard_map/ppermute | solution.py:29
  222.9 24.5 %collective-permute-start.23 = (bf16[2048,256]{1,0:T(8,128)(2,1)S(1)}, bf16[2048,256]{1,0:T(8,128)(2,1)S(1)}, u32[]{:S(2)}, u32[]{:S(2)}) collective-permute-start(bf16[2048,256]{1,0:T(8,128)(2,1)S(1)} %collective-permute-done.21), channel_id=1, source_target_pairs={{0,2},{1,3},{2,4},{3,5},{4,6},{5,7},{6,0},{7,1},{8,10},{9,11},{10,... | collective-permute-start | bytes 3145736 | tf_op jit(solution)/shard_map/ppermute | solution.py:26
  229.1 18.5 %collective-permute-start.13 = (bf16[2048,256]{0,1:T(8,128)(2,1)S(1)}, bf16[2048,256]{0,1:T(8,128)(2,1)S(1)}, u32[]{:S(2)}, u32[]{:S(2)}) collective-permute-start(bf16[2048,256]{0,1:T(8,128)(2,1)S(1)} %get-tuple-element.16), channel_id=1, source_target_pairs={{0,8},{8,0},{16,24},{24,16},{1,9},{9,1},{17,25},{25,17},{2,10},{10... | collective-permute-start | bytes 3145736 | tf_op jit(solution)/shard_map/ppermute | solution.py:29
  247.4 23.5 %collective-permute-start.25 = (bf16[2048,256]{1,0:T(8,128)(2,1)S(1)}, bf16[2048,256]{1,0:T(8,128)(2,1)S(1)}, u32[]{:S(2)}, u32[]{:S(2)}) collective-permute-start(bf16[2048,256]{1,0:T(8,128)(2,1)S(1)} %collective-permute-done.23), channel_id=1, source_target_pairs={{0,2},{1,3},{2,4},{3,5},{4,6},{5,7},{6,0},{7,1},{8,10},{9,11},{10,... | collective-permute-start | bytes 3145736 | tf_op jit(solution)/shard_map/ppermute | solution.py:26
  251.2 23.1 %collective-permute-start.18 = (bf16[2048,256]{0,1:T(8,128)(2,1)S(1)}, bf16[2048,256]{0,1:T(8,128)(2,1)S(1)}, u32[]{:S(2)}, u32[]{:S(2)}) collective-permute-start(bf16[2048,256]{0,1:T(8,128)(2,1)S(1)} %get-tuple-element.14), channel_id=1, source_target_pairs={{0,8},{8,0},{16,24},{24,16},{1,9},{9,1},{17,25},{25,17},{2,10},{10... | collective-permute-start | bytes 3145736 | tf_op jit(solution)/shard_map/ppermute | solution.py:29
  277.0 14.9 %collective-permute-start.26 = (bf16[1024,256]{0,1:T(8,128)(2,1)S(1)}, bf16[1024,256]{0,1:T(8,128)(2,1)S(1)}, u32[]{:S(2)}, u32[]{:S(2)}) collective-permute-start(bf16[1024,256]{0,1:T(8,128)(2,1)S(1)} %fusion.63), channel_id=1, source_target_pairs={{0,1},{1,0},{2,3},{3,2},{4,5},{5,4},{6,7},{7,6},{8,9},{9,8},{10,11... | collective-permute-start | bytes 1572872 | tf_op jit(solution)/shard_map/ppermute | solution.py:26
  279.0 24.2 %collective-permute-start.24 = (bf16[1024,256]{0,1:T(8,128)(2,1)S(1)}, bf16[1024,256]{0,1:T(8,128)(2,1)S(1)}, u32[]{:S(2)}, u32[]{:S(2)}) collective-permute-start(bf16[1024,256]{0,1:T(8,128)(2,1)S(1)} %fusion.60), channel_id=1, source_target_pairs={{0,1},{1,0},{2,3},{3,2},{4,5},{5,4},{6,7},{7,6},{8,9},{9,8},{10,11... | collective-permute-start | bytes 1572872 | tf_op jit(solution)/shard_map/ppermute | solution.py:26
  281.8 32.6 %collective-permute-start.22 = (bf16[1024,256]{0,1:T(8,128)(2,1)S(1)}, bf16[1024,256]{0,1:T(8,128)(2,1)S(1)}, u32[]{:S(2)}, u32[]{:S(2)}) collective-permute-start(bf16[1024,256]{0,1:T(8,128)(2,1)S(1)} %fusion.57), channel_id=1, source_target_pairs={{0,1},{1,0},{2,3},{3,2},{4,5},{5,4},{6,7},{7,6},{8,9},{9,8},{10,11... | collective-permute-start | bytes 1572872 | tf_op jit(solution)/shard_map/ppermute | solution.py:26
  282.4 38.0 %collective-permute-start.20 = (bf16[1024,256]{0,1:T(8,128)(2,1)S(1)}, bf16[1024,256]{0,1:T(8,128)(2,1)S(1)}, u32[]{:S(2)}, u32[]{:S(2)}) collective-permute-start(bf16[1024,256]{0,1:T(8,128)(2,1)S(1)} %fusion.54), channel_id=1, source_target_pairs={{0,1},{1,0},{2,3},{3,2},{4,5},{5,4},{6,7},{7,6},{8,9},{9,8},{10,11... | collective-permute-start | bytes 1572872 | tf_op jit(solution)/shard_map/ppermute | solution.py:26
  331.6 5.0 copy-start.5
  333.6 5.0 copy-start
  334.3 4.3 collective-permute-start.27
  334.4 26.3 %collective-permute-start.31 = (bf16[1024,256]{1,0:T(8,128)(2,1)S(1)}, bf16[1024,256]{1,0:T(8,128)(2,1)S(1)}, u32[]{:S(2)}, u32[]{:S(2)}) collective-permute-start(bf16[1024,256]{1,0:T(8,128)(2,1)S(1)} %get-tuple-element.42), channel_id=1, source_target_pairs={{0,24},{8,16},{16,8},{24,0},{1,25},{9,17},{17,9},{25,1},{2,26},{10... | collective-permute-start | bytes 1572872 | tf_op jit(solution)/shard_map/ppermute | solution.py:29
  336.1 23.8 %collective-permute-start.29 = (bf16[1024,256]{1,0:T(8,128)(2,1)S(1)}, bf16[1024,256]{1,0:T(8,128)(2,1)S(1)}, u32[]{:S(2)}, u32[]{:S(2)}) collective-permute-start(bf16[1024,256]{1,0:T(8,128)(2,1)S(1)} %get-tuple-element.43), channel_id=1, source_target_pairs={{0,16},{8,24},{16,0},{24,8},{1,17},{9,25},{17,1},{25,9},{2,18},{10... | collective-permute-start | bytes 1572872 | tf_op jit(solution)/shard_map/ppermute | solution.py:29
  363.2 27.6 %copy-start.6 = (bf16[2048,256]{1,0:T(8,128)(2,1)S(1)}, bf16[2048,256]{1,0:T(8,128)(2,1)}, u32[]{:S(2)}) copy-start(bf16[2048,256]{1,0:T(8,128)(2,1)} %get-tuple-element.36) | copy-start | bytes 3145732
  363.3 14.2 %collective-permute-start.32 = (bf16[1024,256]{1,0:T(8,128)(2,1)S(1)}, bf16[1024,256]{1,0:T(8,128)(2,1)S(1)}, u32[]{:S(2)}, u32[]{:S(2)}) collective-permute-start(bf16[1024,256]{1,0:T(8,128)(2,1)S(1)} %pad_maximum_fusion.8), channel_id=1, source_target_pairs={{0,24},{8,16},{16,8},{24,0},{1,25},{9,17},{17,9},{25,1},{2,26},{10... | collective-permute-start | bytes 1572872 | tf_op jit(solution)/shard_map/ppermute | solution.py:29
  364.1 24.7 %collective-permute-start.30 = (bf16[1024,256]{1,0:T(8,128)(2,1)S(1)}, bf16[1024,256]{1,0:T(8,128)(2,1)S(1)}, u32[]{:S(2)}, u32[]{:S(2)}) collective-permute-start(bf16[1024,256]{1,0:T(8,128)(2,1)S(1)} %pad_maximum_fusion.7), channel_id=1, source_target_pairs={{0,16},{8,24},{16,0},{24,8},{1,17},{9,25},{17,1},{25,9},{2,18},{10... | collective-permute-start | bytes 1572872 | tf_op jit(solution)/shard_map/ppermute | solution.py:29
  365.1 24.3 %collective-permute-start.28 = (bf16[1024,256]{1,0:T(8,128)(2,1)S(1)}, bf16[1024,256]{1,0:T(8,128)(2,1)S(1)}, u32[]{:S(2)}, u32[]{:S(2)}) collective-permute-start(bf16[1024,256]{1,0:T(8,128)(2,1)S(1)} %pad_maximum_fusion.6), channel_id=1, source_target_pairs={{0,8},{8,0},{16,24},{24,16},{1,9},{9,1},{17,25},{25,17},{2,10},{10... | collective-permute-start | bytes 1572872 | tf_op jit(solution)/shard_map/ppermute | solution.py:29
  366.5 25.1 %collective-permute-start.33 = (bf16[1024,256]{1,0:T(8,128)(2,1)S(1)}, bf16[1024,256]{1,0:T(8,128)(2,1)S(1)}, u32[]{:S(2)}, u32[]{:S(2)}) collective-permute-start(bf16[1024,256]{1,0:T(8,128)(2,1)S(1)} %pad_maximum_fusion.9), channel_id=1, source_target_pairs={{0,1},{1,0},{2,3},{3,2},{4,5},{5,4},{6,7},{7,6},{8,9},{9,8},{10,11... | collective-permute-start | bytes 1572872 | tf_op jit(solution)/shard_map/ppermute | solution.py:26
  377.4 14.3 %collective-permute-start.36 = (bf16[1024,256]{1,0:T(8,128)(2,1)S(1)}, bf16[1024,256]{1,0:T(8,128)(2,1)S(1)}, u32[]{:S(2)}, u32[]{:S(2)}) collective-permute-start(bf16[1024,256]{1,0:T(8,128)(2,1)S(1)} %collective-permute-done.32), channel_id=1, source_target_pairs={{0,1},{1,0},{2,3},{3,2},{4,5},{5,4},{6,7},{7,6},{8,9},{9,8},{10,11... | collective-permute-start | bytes 1572872 | tf_op jit(solution)/shard_map/ppermute | solution.py:26
  388.8 14.8 %collective-permute-start.35 = (bf16[1024,256]{1,0:T(8,128)(2,1)S(1)}, bf16[1024,256]{1,0:T(8,128)(2,1)S(1)}, u32[]{:S(2)}, u32[]{:S(2)}) collective-permute-start(bf16[1024,256]{1,0:T(8,128)(2,1)S(1)} %collective-permute-done.30), channel_id=1, source_target_pairs={{0,1},{1,0},{2,3},{3,2},{4,5},{5,4},{6,7},{7,6},{8,9},{9,8},{10,11... | collective-permute-start | bytes 1572872 | tf_op jit(solution)/shard_map/ppermute | solution.py:26
  389.4 24.7 %collective-permute-start.34 = (bf16[1024,256]{1,0:T(8,128)(2,1)S(1)}, bf16[1024,256]{1,0:T(8,128)(2,1)S(1)}, u32[]{:S(2)}, u32[]{:S(2)}) collective-permute-start(bf16[1024,256]{1,0:T(8,128)(2,1)S(1)} %collective-permute-done.28), channel_id=1, source_target_pairs={{0,1},{1,0},{2,3},{3,2},{4,5},{5,4},{6,7},{7,6},{8,9},{9,8},{10,11... | collective-permute-start | bytes 1572872 | tf_op jit(solution)/shard_map/ppermute | solution.py:26
  426.6 5.2 collective-permute-start.43
  428.0 6.6 collective-permute-start.37
  429.9 6.8 %collective-permute-start.39 = (bf16[2048,256]{1,0:T(8,128)(2,1)S(1)}, bf16[2048,256]{1,0:T(8,128)(2,1)S(1)}, u32[]{:S(2)}, u32[]{:S(2)}) collective-permute-start(bf16[2048,256]{1,0:T(8,128)(2,1)S(1)} %convolution_convert_fusion.2), channel_id=1, source_target_pairs={{0,8},{8,0},{16,24},{24,16},{1,9},{9,1},{17,25},{25,17},{2,10},{10... | collective-permute-start | bytes 3145736 | tf_op jit(solution)/shard_map/ppermute | solution.py:29
  431.2 8.3 %collective-permute-start.41 = (bf16[2048,256]{1,0:T(8,128)(2,1)S(1)}, bf16[2048,256]{1,0:T(8,128)(2,1)S(1)}, u32[]{:S(2)}, u32[]{:S(2)}) collective-permute-start(bf16[2048,256]{1,0:T(8,128)(2,1)S(1)} %convolution_convert_fusion.1), channel_id=1, source_target_pairs={{0,8},{8,0},{16,24},{24,16},{1,9},{9,1},{17,25},{25,17},{2,10},{10... | collective-permute-start | bytes 3145736 | tf_op jit(solution)/shard_map/ppermute | solution.py:29
  433.2 26.1 %collective-permute-start.44 = (bf16[2048,256]{1,0:T(8,128)(2,1)S(1)}, bf16[2048,256]{1,0:T(8,128)(2,1)S(1)}, u32[]{:S(2)}, u32[]{:S(2)}) collective-permute-start(bf16[2048,256]{1,0:T(8,128)(2,1)S(1)} %fusion.29), channel_id=1, source_target_pairs={{0,16},{8,24},{16,0},{24,8},{1,17},{9,25},{17,1},{25,9},{2,18},{10... | collective-permute-start | bytes 3145736 | tf_op jit(solution)/shard_map/ppermute | solution.py:29
  436.0 142.9 %collective-permute-start.38 = (bf16[2048,256]{1,0:T(8,128)(2,1)S(1)}, bf16[2048,256]{1,0:T(8,128)(2,1)S(1)}, u32[]{:S(2)}, u32[]{:S(2)}) collective-permute-start(bf16[2048,256]{1,0:T(8,128)(2,1)S(1)} %fusion.26), channel_id=1, source_target_pairs={{0,16},{8,24},{16,0},{24,8},{1,17},{9,25},{17,1},{25,9},{2,18},{10... | collective-permute-start | bytes 3145736 | tf_op jit(solution)/shard_map/ppermute | solution.py:29
  436.7 22.9 %slice-start = ((s8[8388608]{0:T(1024)(128)(4,1)}), s8[4194304]{0:T(1024)(128)(4,1)S(1)}, s32[]{:S(2)}) async-start(s8[8388608]{0:T(1024)(128)(4,1)} %bitcast.81), calls=%async_computation.1 | async-start | bytes 8388608
  438.1 21.6 %slice-start.1 = ((s8[8388608]{0:T(1024)(128)(4,1)}), s8[4194304]{0:T(1024)(128)(4,1)S(1)}, s32[]{:S(2)}) async-start(s8[8388608]{0:T(1024)(128)(4,1)} %bitcast.81), calls=%async_computation.2 | async-start | bytes 8388608
  438.1 90.6 %collective-permute-start.40 = (bf16[2048,256]{1,0:T(8,128)(2,1)S(1)}, bf16[2048,256]{1,0:T(8,128)(2,1)S(1)}, u32[]{:S(2)}, u32[]{:S(2)}) collective-permute-start(bf16[2048,256]{1,0:T(8,128)(2,1)S(1)} %fusion.27), channel_id=1, source_target_pairs={{0,16},{8,24},{16,0},{24,8},{1,17},{9,25},{17,1},{25,9},{2,18},{10... | collective-permute-start | bytes 3145736 | tf_op jit(solution)/shard_map/ppermute | solution.py:29
  440.9 84.8 %collective-permute-start.42 = (bf16[2048,256]{1,0:T(8,128)(2,1)S(1)}, bf16[2048,256]{1,0:T(8,128)(2,1)S(1)}, u32[]{:S(2)}, u32[]{:S(2)}) collective-permute-start(bf16[2048,256]{1,0:T(8,128)(2,1)S(1)} %fusion.28), channel_id=1, source_target_pairs={{0,16},{8,24},{16,0},{24,8},{1,17},{9,25},{17,1},{25,9},{2,18},{10... | collective-permute-start | bytes 3145736 | tf_op jit(solution)/shard_map/ppermute | solution.py:29
  459.5 66.6 %collective-permute-start.51 = (bf16[2048,256]{1,0:T(8,128)(2,1)S(1)}, bf16[2048,256]{1,0:T(8,128)(2,1)S(1)}, u32[]{:S(2)}, u32[]{:S(2)}) collective-permute-start(bf16[2048,256]{1,0:T(8,128)(2,1)S(1)} %add_convert_fusion), channel_id=1, source_target_pairs={{0,8},{8,0},{16,24},{24,16},{1,9},{9,1},{17,25},{25,17},{2,10},{10... | collective-permute-start | bytes 3145736 | tf_op jit(solution)/shard_map/ppermute | solution.py:29
  526.0 30.4 %collective-permute-start.50 = (bf16[2048,256]{1,0:T(8,128)(2,1)S(1)}, bf16[2048,256]{1,0:T(8,128)(2,1)S(1)}, u32[]{:S(2)}, u32[]{:S(2)}) collective-permute-start(bf16[2048,256]{1,0:T(8,128)(2,1)S(1)} %add_convert_fusion.1), channel_id=1, source_target_pairs={{0,8},{8,0},{16,24},{24,16},{1,9},{9,1},{17,25},{25,17},{2,10},{10... | collective-permute-start | bytes 3145736 | tf_op jit(solution)/shard_map/ppermute | solution.py:29
  526.1 27.8 %collective-permute-start.45 = (bf16[2048,256]{0,1:T(8,128)(2,1)S(1)}, bf16[2048,256]{0,1:T(8,128)(2,1)S(1)}, u32[]{:S(2)}, u32[]{:S(2)}) collective-permute-start(bf16[2048,256]{0,1:T(8,128)(2,1)S(1)} %convolution_convert_fusion.5), channel_id=1, source_target_pairs={{0,2},{1,3},{2,4},{3,5},{4,6},{5,7},{6,0},{7,1},{8,10},{9,11},{10,... | collective-permute-start | bytes 3145736 | tf_op jit(solution)/shard_map/ppermute | solution.py:26
  528.6 47.8 %collective-permute-start.52 = (bf16[2048,256]{0,1:T(8,128)(2,1)S(1)}, bf16[2048,256]{0,1:T(8,128)(2,1)S(1)}, u32[]{:S(2)}, u32[]{:S(2)}) collective-permute-start(bf16[2048,256]{0,1:T(8,128)(2,1)S(1)} %convolution_convert_fusion.4), channel_id=1, source_target_pairs={{0,2},{1,3},{2,4},{3,5},{4,6},{5,7},{6,0},{7,1},{8,10},{9,11},{10,... | collective-permute-start | bytes 3145736 | tf_op jit(solution)/shard_map/ppermute | solution.py:26
  529.0 72.6 %collective-permute-start.49 = (bf16[2048,256]{1,0:T(8,128)(2,1)S(1)}, bf16[2048,256]{1,0:T(8,128)(2,1)S(1)}, u32[]{:S(2)}, u32[]{:S(2)}) collective-permute-start(bf16[2048,256]{1,0:T(8,128)(2,1)S(1)} %add_convert_fusion.2), channel_id=1, source_target_pairs={{0,8},{8,0},{16,24},{24,16},{1,9},{9,1},{17,25},{25,17},{2,10},{10... | collective-permute-start | bytes 3145736 | tf_op jit(solution)/shard_map/ppermute | solution.py:29
  556.3 42.5 %collective-permute-start.46 = (bf16[2048,256]{0,1:T(8,128)(2,1)S(1)}, bf16[2048,256]{0,1:T(8,128)(2,1)S(1)}, u32[]{:S(2)}, u32[]{:S(2)}) collective-permute-start(bf16[2048,256]{0,1:T(8,128)(2,1)S(1)} %fusion.22), channel_id=1, source_target_pairs={{0,2},{1,3},{2,4},{3,5},{4,6},{5,7},{6,0},{7,1},{8,10},{9,11},{10,... | collective-permute-start | bytes 3145736 | tf_op jit(solution)/shard_map/ppermute | solution.py:26
  578.8 42.5 %collective-permute-start.53 = (bf16[2048,256]{0,1:T(8,128)(2,1)S(1)}, bf16[2048,256]{0,1:T(8,128)(2,1)S(1)}, u32[]{:S(2)}, u32[]{:S(2)}) collective-permute-start(bf16[2048,256]{0,1:T(8,128)(2,1)S(1)} %fusion.25), channel_id=1, source_target_pairs={{0,2},{1,3},{2,4},{3,5},{4,6},{5,7},{6,0},{7,1},{8,10},{9,11},{10,... | collective-permute-start | bytes 3145736 | tf_op jit(solution)/shard_map/ppermute | solution.py:26
  579.1 70.8 %collective-permute-start.48 = (bf16[2048,256]{1,0:T(8,128)(2,1)S(1)}, bf16[2048,256]{1,0:T(8,128)(2,1)S(1)}, u32[]{:S(2)}, u32[]{:S(2)}) collective-permute-start(bf16[2048,256]{1,0:T(8,128)(2,1)S(1)} %add_convert_fusion.3), channel_id=1, source_target_pairs={{0,8},{8,0},{16,24},{24,16},{1,9},{9,1},{17,25},{25,17},{2,10},{10... | collective-permute-start | bytes 3145736 | tf_op jit(solution)/shard_map/ppermute | solution.py:29
  601.3 42.6 %collective-permute-start.47 = (bf16[2048,256]{0,1:T(8,128)(2,1)S(1)}, bf16[2048,256]{0,1:T(8,128)(2,1)}, u32[]{:S(2)}, u32[]{:S(2)}) collective-permute-start(bf16[2048,256]{0,1:T(8,128)(2,1)S(1)} %fusion.21), channel_id=1, source_target_pairs={{0,2},{1,3},{2,4},{3,5},{4,6},{5,7},{6,0},{7,1},{8,10},{9,11},{10,... | collective-permute-start | bytes 3145736 | tf_op jit(solution)/shard_map/ppermute | solution.py:26
  624.7 41.2 %collective-permute-start.54 = (bf16[2048,256]{0,1:T(8,128)(2,1)}, bf16[2048,256]{0,1:T(8,128)(2,1)}, u32[]{:S(2)}, u32[]{:S(2)}) collective-permute-start(bf16[2048,256]{0,1:T(8,128)(2,1)} %fusion.24), channel_id=1, source_target_pairs={{0,2},{1,3},{2,4},{3,5},{4,6},{5,7},{6,0},{7,1},{8,10},{9,11},{10,... | collective-permute-start | bytes 3145736 | tf_op jit(solution)/shard_map/ppermute | solution.py:26
  (5 other events, 19.0 us)
Sparse Core Ops, SparseCore 0:
  62.5 35.0 all-gather.1

commit v2 on v1

v2 whole, which is shorter than its diff:
```python
import functools

import jax
import jax.numpy as jnp
from jax import lax
from jax.experimental import pallas as pl
from jax.experimental.pallas import tpu as pltpu
from jax.sharding import PartitionSpec as P

BF16 = jnp.bfloat16
F32 = jnp.float32


def dot(a, b, contract):
    return lax.dot_general(a, b, ((contract[:1], contract[1:]), ((), ())), preferred_element_type=F32)


def tie(x, *earlier):
    return lax.optimization_barrier((x, *earlier))[0]


def moments(first, second, rot):
    first = 0.9 * first + 0.1 * rot
    second = 0.95 * second + 0.05 * rot * rot
    return first, second, (first / (jnp.sqrt(second) + 1e-08)).astype(BF16)


def moments_kernel(peer_ref, rot_ref, first_ref, second_ref, *refs):
    first_new, second_new, direction = refs[-3:]
    first_new[...], second_new[...], direction[...] = moments(
        first_ref[...], second_ref[...], rot_ref[0].astype(F32)
    )


def moments_at(peer, n_row, sub, rot, first_moment, second_moment, before):
    blocks, rows, _ = rot.shape
    block = min(rows, 512)
    packed_rot = pl.BlockSpec((1, block, sub), lambda q, i, p: (q, i, 0))
    at_peer = pl.BlockSpec((block, sub), lambda q, i, p: (i, q * n_row + p[0]))
    packed = pl.BlockSpec((block, sub), lambda q, i, p: (i, q))
    kept = [pl.BlockSpec(memory_space=pl.ANY)] * len(before)
    out = jax.ShapeDtypeStruct(first_moment.shape, F32)
    return pl.pallas_call(
        moments_kernel,
        grid_spec=pltpu.PrefetchScalarGridSpec(
            num_scalar_prefetch=1,
            grid=(blocks, rows // block),
            in_specs=[packed_rot, at_peer, at_peer] + kept,
            out_specs=[at_peer, at_peer, packed],
        ),
        out_shape=[out, out, jax.ShapeDtypeStruct((rows, blocks * sub), BF16)],
        input_output_aliases={4: 0, 5: 1} if before else {},
        cost_estimate=pl.CostEstimate(
            flops=10 * rot.size, bytes_accessed=20 * rot.size, transcendentals=2 * rot.size
        ),
    )(peer.reshape(1), rot, first_moment, second_moment, *before)


def moments_sliced(peer, n_row, sub, rot, first_moment, second_moment, before):
    first_new, second_new = before if before else (first_moment, second_moment)
    directions = []
    for q in range(rot.shape[0]):
        start = (q * n_row + peer) * sub
        first, second, direction = moments(
            lax.dynamic_slice_in_dim(first_moment, start, sub, 1),
            lax.dynamic_slice_in_dim(second_moment, start, sub, 1),
            rot[q].astype(F32),
        )
        first_new = lax.dynamic_update_slice_in_dim(first_new, first, start, 1)
        second_new = lax.dynamic_update_slice_in_dim(second_new, second, start, 1)
        directions.append(direction)
    return first_new, second_new, jnp.concatenate(directions, axis=1)


def solution(mesh):
    n_row, n_col = mesh.shape["row"], mesh.shape["col"]
    n_a = 4 if n_col % 4 == 0 else n_col
    n_b = n_col // n_a
    per_row = n_col // n_row

    def b_shift(x, db):
        perm = [(a * n_b + b, a * n_b + (b + db) % n_b) for a in range(n_a) for b in range(n_b)]
        return lax.ppermute(x, "col", perm)

    def a_shift(x, mine):
        perm = []
        for r in range(n_row):
            up = (r % 2 == 0) == mine
            for a in range(n_a):
                for b in range(n_b):
                    to = (a + (1 if up else -1)) % n_a
                    perm.append((r * n_col + a * n_b + b, r * n_col + to * n_b + b))
        return lax.ppermute(x, ("row", "col"), perm)

    def a_shift_up(x, up):
        perm = [
            (a * n_b + b, ((a + (1 if up else -1)) % n_a) * n_b + b) for a in range(n_a) for b in range(n_b)
        ]
        return lax.ppermute(x, "col", perm)

    def row_xor(x, k):
        return lax.ppermute(x, "row", [(r, r ^ k) for r in range(n_row)])

    def half_sum(theirs, mine, gate=()):
        got = row_xor(theirs().astype(BF16), 1)
        mine = (mine() + got.astype(F32)).astype(BF16)
        if gate:
            mine = tie(mine, *gate)
        k = 2
        while k < n_row:
            mine = (mine.astype(F32) + row_xor(mine, k).astype(F32)).astype(BF16)
            k *= 2
        return mine, row_xor(mine, 1)

    def per_device(grad, basis_left, basis_right, first_moment, second_moment):
        r = lax.axis_index("row")
        c = lax.axis_index("col")
        a, b = c // n_b, c % n_b
        core = r % 2
        width = grad.shape[1]
        half = width // 2
        sub = width // n_row
        own_i = basis_left.shape[1]
        row_n = basis_right.shape[0]

        def block_of(s, h):
            return (a + (2 * h - 1) * s) % n_a

        g_theirs = [lax.dynamic_slice_in_dim(grad, (1 - core) * half, half, 1)]
        g_mine = [lax.dynamic_slice_in_dim(grad, core * half, half, 1)]
        g_theirs.append(a_shift(g_theirs[0], False))
        g_mine.append(a_shift(g_mine[0], True))

        right_after = tie(basis_right, g_theirs[0], g_mine[0])
        right_n = jnp.zeros((n_row * row_n, sub), BF16)
        for k in range(n_row):
            part = lax.dynamic_slice_in_dim(right_after, (r ^ k) * sub, sub, 1)
            if k:
                part = row_xor(part, k)
            right_n = lax.dynamic_update_slice_in_dim(right_n, part, (r ^ k) * row_n, 0)
        by_b = right_n.reshape(n_a, n_b, width, sub)

        def rows_of(which):
            return lax.dynamic_index_in_dim(by_b, which, 1, keepdims=False).reshape(n_a * width, sub)

        got = [rows_of(b)] + [b_shift(rows_of((b + k) % n_b), k) for k in range(1, n_b)]

        lefts = [basis_left] + [b_shift(tie(basis_left, g_theirs[0], g_mine[0]), -k) for k in range(1, n_b)]
        lefts = list(tie(tuple(lefts), g_theirs[1], g_mine[1]))
        left = jnp.concatenate(lefts, axis=1)

        for s in range(2, n_a):
            g_theirs.append(a_shift(g_theirs[-1], False))
            g_mine.append(a_shift(g_mine[-1], True))

        got = tie(tuple(got), g_theirs[2], g_mine[2])
        stacked = jnp.stack(got, 0)
        right_b = [lax.dynamic_index_in_dim(stacked, (b - q) % n_b, 0, keepdims=False) for q in range(n_b)]
        right_up = jnp.concatenate(right_b[: n_b // 2], axis=1)
        right_down = jnp.concatenate(right_b[n_b // 2 :], axis=1)

        def n_at(s, h):
            return block_of(s, h) * width + h * half

        left_rotated = jnp.zeros((n_b * own_i, n_a * width), BF16)
        for s in range(n_a):
            mine, theirs = half_sum(
                lambda: dot(left, g_theirs[s], (0, 0)),
                lambda: dot(left, g_mine[s], (0, 0)),
            )
            left_rotated = lax.dynamic_update_slice_in_dim(left_rotated, mine, n_at(s, core), 1)
            left_rotated = lax.dynamic_update_slice_in_dim(left_rotated, theirs, n_at(s, 1 - core), 1)

        rot_k = jnp.zeros((n_col, own_i, sub), BF16)
        right_k = jnp.zeros((n_a * width, n_col * sub), BF16)
        for t in range(n_a):
            if t:
                right_up, right_down = a_shift_up(right_up, True), a_shift_up(right_down, False)
            right_t = jnp.concatenate([right_up, right_down], axis=1)
            rot = dot(left_rotated[:own_i], right_t, (1, 0))
            for k in range(1, n_b):
                part = dot(left_rotated[k * own_i : (k + 1) * own_i], right_t, (1, 0))
                rot = rot + b_shift(part.astype(BF16), k).astype(F32)
            rot = rot.astype(BF16)
            for q in range(n_b):
                block = block_of(t, 2 * q // n_b) * n_b + q
                at = (block // per_row ^ r) * per_row + block % per_row
                columns = slice(q * sub, (q + 1) * sub)
                rot_k = lax.dynamic_update_index_in_dim(rot_k, rot[:, columns], at, 0)
                right_k = lax.dynamic_update_slice_in_dim(right_k, right_t[:, columns], at * sub, 1)

        step = moments_at if sub % 128 == 0 else moments_sliced
        kept, directions = (), []
        for k in range(n_row):
            rot = rot_k[k * per_row : (k + 1) * per_row]
            if k:
                rot = row_xor(rot, k)
            *kept, direction = step(r ^ k, n_row, sub, rot, first_moment, second_moment, tuple(kept))
            if k:
                direction = row_xor(direction, k)
            directions.append(direction)
        first_new, second_new = kept

        by_rows = [directions] + [[b_shift(d, -k) for d in directions] for k in range(1, n_b)]
        by_rows = [jnp.concatenate(ds, axis=1) for ds in by_rows]

        u_mine = u_theirs = None
        gates = []
        for s in list(range(1, n_a)) + [0]:
            r_mine = lax.dynamic_slice_in_dim(right_k, n_at(s, core), half, 0)
            r_theirs = lax.dynamic_slice_in_dim(right_k, n_at(s, 1 - core), half, 0)
            new_mine = new_theirs = 0.0
            for k in range(n_b):
                w_mine, w_theirs = half_sum(
                    lambda: dot(by_rows[k], r_theirs, (1, 1)), lambda: dot(by_rows[k], r_mine, (1, 1)), gates[-2:-1]
                )
                gates.append(w_mine)
                new_mine = new_mine + dot(lefts[k], w_mine, (1, 0))
                new_theirs = new_theirs + dot(lefts[k], w_theirs, (1, 0))
            if u_mine is not None:
                new_mine = new_mine + a_shift(u_mine, True).astype(F32)
                new_theirs = new_theirs + a_shift(u_theirs, False).astype(F32)
            u_mine, u_theirs = new_mine.astype(BF16), new_theirs.astype(BF16)
        update = jnp.where(
            core == 0,
            jnp.concatenate([u_mine, u_theirs], axis=1),
            jnp.concatenate([u_theirs, u_mine], axis=1),
        )
        return update, first_new, second_new

    in_specs = (P("row", "col"), P("row", "col"), P("row", "col"), P("col", "row"), P("col", "row"))
    out_specs = (P("row", "col"), P("col", "row"), P("col", "row"))
    return jax.shard_map(per_device, mesh=mesh, in_specs=in_specs, out_specs=out_specs, check_vma=False)
```

time: 693 us -> 655 us (0.945)
  waiting for transfers between devices: 505 us -> 361 us
  starting transfers between devices: 31.8 us -> 109 us
  matrix products: 76 us -> 120 us
  other arithmetic: 30.4 us -> 7.08 us
  Pallas kernels: 0 us -> 16.5 us
  between operations: 15.9 us -> 1.84 us
  local copies, waits for them, and re-layouts: 23.7 us -> 31.1 us
    ppermute x25 -> x28, waiting for transfers between devices: 351 us -> 232 us  [the longest x10 117 us: b_shift(): return lax.ppermute(x, 'col', perm)]
    ppermute x25 -> x28, starting transfers between devices: 14.9 us -> 86.1 us  [the longest x12 57.1 us: a_shift(): return lax.ppermute(x, ('row', 'col'), perm)]
    dot_general x32 -> x48, matrix products: 76 us -> 120 us  [dot(): lax.dot_general(a, b, ((contract[:1], contract[1:]), ((), ())), preferred...]
    ppermute x30 -> x45, waiting for transfers between devices: 154 us -> 129 us  [row_xor(): return lax.ppermute(x, 'row', [(r, r ^ k) for r in range(n_row)])]
    pallas_call x0 -> x4, Pallas kernels: none -> 16.5 us  [moments_at(): pl.pallas_call(moments_kernel, grid_spec=pltpu.PrefetchScalarGridSpec(num...]
    concatenate x10 -> x0, other arithmetic: 15 us -> none  [the longest x1 11.2 us: per_device(): direction = jnp.concatenate(rows, axis=0)]
    dynamic_update_slice x0 -> x21, local copies, waits for them, and re-layouts: none -> 10.8 us  [the longest x6 6.65 us: per_device(): lax.dynamic_update_slice_in_dim(right_k, right_t[:, columns], at * sub, 1)]
    dynamic_slice x8 -> x2, local copies, waits for them, and re-layouts: 14.3 us -> 3.63 us  [the longest x1 2.73 us: per_device(): g_mine = [lax.dynamic_slice_in_dim(grad, core * half, half, 1)]]
  transfers between devices with their start and end apart: 56 -> 73, of which waited for: 31 -> 36; matrix products, arithmetic and copies ran while one was open for 13% -> 21% of each run, Pallas kernels for 0% -> 3%
where the time goes in v2:
time: 655 us; the launch traced here: 646 us
  waiting for transfers between devices  361 us (55%)
  matrix products  120 us (18%)
  starting transfers between devices  109 us (17%)
  local copies, waits for them, and re-layouts  31.1 us (5%)
  Pallas kernels  16.5 us (3%)
  other arithmetic  7.08 us (1%)
    ppermute x45, waiting for transfers between devices, row_xor(): return lax.ppermute(x, 'row', [(r, r ^ k) for r in range(n_row)])  129 us
    dot_general x48, matrix products, dot(): lax.dot_general(a, b, ((contract[:1], contract[1:]), ((), ())), preferred...  120 us
    ppermute x10, waiting for transfers between devices, b_shift(): return lax.ppermute(x, 'col', perm)  117 us
    ppermute x12, waiting for transfers between devices, a_shift(): return lax.ppermute(x, ('row', 'col'), perm)  79.1 us
    ppermute x12, starting transfers between devices, a_shift(): return lax.ppermute(x, ('row', 'col'), perm)  57.1 us
    ppermute x6, waiting for transfers between devices, a_shift_up(): return lax.ppermute(x, 'col', perm)  36.3 us
    ppermute x45, starting transfers between devices, row_xor(): return lax.ppermute(x, 'row', [(r, r ^ k) for r in range(n_row)])  22.5 us
    pallas_call x4, Pallas kernels, moments_at(): pl.pallas_call(moments_kernel, grid_spec=pltpu.PrefetchScalarGridSpec(num...  16.5 us
  transfers between devices with their start and end apart: 73, of which 36 were waited for; matrix products, arithmetic and copies ran while one was open for 21% of the time, Pallas kernels for 3%

profile of v2, /device:TPU:0, one launch (start us, length us, event | category | flops | bytes accessed | tf_op | source)
XLA Modules:
  0.0 646.1 jit_solution(5287834002182819828)
XLA Ops:
  12.7 21.7 %collective-permute-done.2 = bf16[2048,256]{1,0:T(8,128)(2,1)} collective-permute-done((bf16[2048,256]{1,0:T(8,128)(2,1)S(1)}, bf16[2048,256]{1,0:T(8,128)(2,1)}, u32[]{:S(2)}, u32[]{:S(2)}) %collective-permute-start.2) | collective-permute-done | bytes 1048608 | tf_op jit(solution)/shard_map/ppermute | solution.py:93
  34.4 19.5 %collective-permute-start.9 = (bf16[2048,256]{1,0:T(8,128)(2,1)}, bf16[2048,256]{1,0:T(8,128)(2,1)}, u32[]{:S(2)}, u32[]{:S(2)}) collective-permute-start(bf16[2048,256]{1,0:T(8,128)(2,1)} %collective-permute-done.2), channel_id=1, source_target_pairs={{0,2},{1,3},{2,4},{3,5},{4,6},{5,7},{6,0},{7,1},{8,14},{9,15},{10,... | collective-permute-start | bytes 3145736 | tf_op jit(solution)/shard_map/ppermute | solution.py:93
  54.2 3.5 collective-permute-start.10
  57.8 39.5 %collective-permute-done = bf16[2048,1024]{1,0:T(8,128)(2,1)} collective-permute-done((bf16[2048,1024]{1,0:T(8,128)(2,1)}, bf16[2048,1024]{1,0:T(8,128)(2,1)}, u32[]{:S(2)}, u32[]{:S(2)}) %collective-permute-start) | collective-permute-done | bytes 4194336 | tf_op jit(solution)/shard_map/ppermute | solution.py:83
  102.5 5.6 convolution_convert_fusion.3
  110.1 6.3 collective-permute-done.21
  118.9 12.7 %collective-permute-done.22 = bf16[2048,128]{1,0:T(8,128)(2,1)S(1)} collective-permute-done((bf16[2048,128]{1,0:T(8,128)(2,1)}, bf16[2048,128]{1,0:T(8,128)(2,1)S(1)}, u32[]{:S(2)}, u32[]{:S(2)}) %collective-permute-start.22) | collective-permute-done | bytes 524320 | tf_op jit(solution)/shard_map/ppermute | solution.py:83
  135.7 6.2 fusion.22
  143.6 4.9 convolution_convert_fusion.2
  148.5 3.9 convolution_convert_fusion.1
  153.0 13.3 %collective-permute-done.4 = bf16[2048,256]{1,0:T(8,128)(2,1)S(1)} collective-permute-done((bf16[2048,256]{1,0:T(8,128)(2,1)S(1)}, bf16[2048,256]{1,0:T(8,128)(2,1)S(1)}, u32[]{:S(2)}, u32[]{:S(2)}) %collective-permute-start.4) | collective-permute-done | bytes 1048608 | tf_op jit(solution)/shard_map/ppermute | solution.py:102
  167.8 4.3 fusion.23
  173.6 4.5 fusion.24
  178.9 19.2 %collective-permute-done.7 = bf16[2048,256]{1,0:T(8,128)(2,1)S(1)} collective-permute-done((bf16[2048,256]{1,0:T(8,128)(2,1)S(1)}, bf16[2048,256]{1,0:T(8,128)(2,1)S(1)}, u32[]{:S(2)}, u32[]{:S(2)}) %collective-permute-start.7) | collective-permute-done | bytes 1048608 | tf_op jit(solution)/shard_map/ppermute | solution.py:102
  198.6 4.1 convolution_convert_fusion
  205.3 14.9 %collective-permute-done.12 = bf16[2048,256]{1,0:T(8,128)(2,1)S(1)} collective-permute-done((bf16[2048,256]{1,0:T(8,128)(2,1)S(1)}, bf16[2048,256]{1,0:T(8,128)(2,1)S(1)}, u32[]{:S(2)}, u32[]{:S(2)}) %collective-permute-start.12) | collective-permute-done | bytes 1048608 | tf_op jit(solution)/shard_map/ppermute | solution.py:102
  220.7 4.6 fusion.25
  230.0 3.5 collective-permute-start.25
  233.5 12.6 %collective-permute-done.25 = bf16[2048,128]{1,0:T(8,128)(2,1)S(1)} collective-permute-done((bf16[2048,128]{1,0:T(8,128)(2,1)}, bf16[2048,128]{1,0:T(8,128)(2,1)S(1)}, u32[]{:S(2)}, u32[]{:S(2)}) %collective-permute-start.25) | collective-permute-done | bytes 524320 | tf_op jit(solution)/shard_map/ppermute | solution.py:99
  246.2 4.2 collective-permute-start.28
  252.4 5.4 collective-permute-done.27
  268.9 4.4 collective-permute-start.31
  275.1 5.1 collective-permute-done.30
  281.3 9.7 %collective-permute-done.31 = bf16[2048,128]{1,0:T(8,128)(2,1)S(1)} collective-permute-done((bf16[2048,128]{1,0:T(8,128)(2,1)S(1)}, bf16[2048,128]{1,0:T(8,128)(2,1)S(1)}, u32[]{:S(2)}, u32[]{:S(2)}) %collective-permute-start.31) | collective-permute-done | bytes 524320 | tf_op jit(solution)/shard_map/ppermute | solution.py:99
  293.0 3.7 fusion.66
  305.3 6.3 collective-permute-done.23
  313.9 8.9 %collective-permute-done.26 = bf16[1024,256]{1,0:T(8,128)(2,1)S(1)} collective-permute-done((bf16[1024,256]{1,0:T(8,128)(2,1)S(1)}, bf16[1024,256]{1,0:T(8,128)(2,1)S(1)}, u32[]{:S(2)}, u32[]{:S(2)}) %collective-permute-start.26) | collective-permute-done | bytes 524320 | tf_op jit(solution)/shard_map/ppermute | solution.py:83
  324.5 9.6 %collective-permute-done.29 = bf16[1024,256]{1,0:T(8,128)(2,1)S(1)} collective-permute-done((bf16[1024,256]{1,0:T(8,128)(2,1)S(1)}, bf16[1024,256]{1,0:T(8,128)(2,1)S(1)}, u32[]{:S(2)}, u32[]{:S(2)}) %collective-permute-start.29) | collective-permute-done | bytes 524320 | tf_op jit(solution)/shard_map/ppermute | solution.py:83
  335.5 8.9 %collective-permute-done.32 = bf16[1024,256]{1,0:T(8,128)(2,1)S(1)} collective-permute-done((bf16[1024,256]{1,0:T(8,128)(2,1)S(1)}, bf16[1024,256]{1,0:T(8,128)(2,1)S(1)}, u32[]{:S(2)}, u32[]{:S(2)}) %collective-permute-start.32) | collective-permute-done | bytes 524320 | tf_op jit(solution)/shard_map/ppermute | solution.py:83
  348.7 4.1 shard_map.76
  355.1 4.1 shard_map.77
  362.3 4.1 shard_map.78
  366.9 5.1 collective-permute-done.37.rot_ref
  372.8 4.3 shard_map.79
  378.1 5.9 collective-permute-done.36
  384.1 10.4 %collective-permute-done.38 = bf16[1024,256]{1,0:T(8,128)(2,1)S(1)} collective-permute-done((bf16[1024,256]{1,0:T(8,128)(2,1)}, bf16[1024,256]{1,0:T(8,128)(2,1)S(1)}, u32[]{:S(2)}, u32[]{:S(2)}) %collective-permute-start.38) | collective-permute-done | bytes 524320 | tf_op jit(solution)/shard_map/ppermute | solution.py:102
  401.7 9.2 %collective-permute-done.48 = bf16[1024,256]{1,0:T(8,128)(2,1)S(1)} collective-permute-done((bf16[1024,256]{1,0:T(8,128)(2,1)S(1)}, bf16[1024,256]{1,0:T(8,128)(2,1)S(1)}, u32[]{:S(2)}, u32[]{:S(2)}) %collective-permute-start.48) | collective-permute-done | bytes 524320 | tf_op jit(solution)/shard_map/ppermute | solution.py:83
  411.0 11.2 %collective-permute-done.49 = bf16[1024,256]{1,0:T(8,128)(2,1)S(1)} collective-permute-done((bf16[1024,256]{1,0:T(8,128)(2,1)S(1)}, bf16[1024,256]{1,0:T(8,128)(2,1)S(1)}, u32[]{:S(2)}, u32[]{:S(2)}) %collective-permute-start.49) | collective-permute-done | bytes 524320 | tf_op jit(solution)/shard_map/ppermute | solution.py:83
  422.2 10.4 %collective-permute-done.50 = bf16[1024,256]{1,0:T(8,128)(2,1)S(1)} collective-permute-done((bf16[1024,256]{1,0:T(8,128)(2,1)S(1)}, bf16[1024,256]{1,0:T(8,128)(2,1)S(1)}, u32[]{:S(2)}, u32[]{:S(2)}) %collective-permute-start.50) | collective-permute-done | bytes 524320 | tf_op jit(solution)/shard_map/ppermute | solution.py:83
  443.0 11.1 %collective-permute-done.43 = bf16[1024,256]{1,0:T(8,128)(2,1)S(1)} collective-permute-done((bf16[1024,256]{1,0:T(8,128)(2,1)S(1)}, bf16[1024,256]{1,0:T(8,128)(2,1)S(1)}, u32[]{:S(2)}, u32[]{:S(2)}) %collective-permute-start.43) | collective-permute-done | bytes 524320 | tf_op jit(solution)/shard_map/ppermute | solution.py:102
  457.5 7.9 %collective-permute-done.55 = bf16[1024,256]{1,0:T(8,128)(2,1)S(1)} collective-permute-done((bf16[1024,256]{1,0:T(8,128)(2,1)S(1)}, bf16[1024,256]{1,0:T(8,128)(2,1)S(1)}, u32[]{:S(2)}, u32[]{:S(2)}) %collective-permute-start.55) | collective-permute-done | bytes 524320 | tf_op jit(solution)/shard_map/ppermute | solution.py:102
  469.7 6.9 %collective-permute-done.44 = bf16[1024,256]{1,0:T(8,128)(2,1)S(1)} collective-permute-done((bf16[1024,256]{1,0:T(8,128)(2,1)S(1)}, bf16[1024,256]{1,0:T(8,128)(2,1)S(1)}, u32[]{:S(2)}, u32[]{:S(2)}) %collective-permute-start.44) | collective-permute-done | bytes 524320 | tf_op jit(solution)/shard_map/ppermute | solution.py:102
  477.5 3.5 fusion.32
  481.0 6.9 %collective-permute-done.56 = bf16[1024,256]{1,0:T(8,128)(2,1)S(1)} collective-permute-done((bf16[1024,256]{1,0:T(8,128)(2,1)S(1)}, bf16[1024,256]{1,0:T(8,128)(2,1)S(1)}, u32[]{:S(2)}, u32[]{:S(2)}) %collective-permute-start.56) | collective-permute-done | bytes 524320 | tf_op jit(solution)/shard_map/ppermute | solution.py:102
  488.6 3.5 fusion.129
  492.1 6.1 collective-permute-done.45
  503.0 3.5 fusion.33
  506.5 4.7 collective-permute-done.57
  511.8 3.5 fusion.128
  515.3 7.9 %collective-permute-done.46 = bf16[1024,256]{1,0:T(8,128)(2,1)S(1)} collective-permute-done((bf16[1024,256]{1,0:T(8,128)(2,1)S(1)}, bf16[1024,256]{1,0:T(8,128)(2,1)S(1)}, u32[]{:S(2)}, u32[]{:S(2)}) %collective-permute-start.46) | collective-permute-done | bytes 524320 | tf_op jit(solution)/shard_map/ppermute | solution.py:102
  530.9 3.5 fusion.29
  534.7 13.5 %collective-permute-done.70 = bf16[2048,256]{0,1:T(8,128)(2,1)S(1)} collective-permute-done((bf16[2048,256]{0,1:T(8,128)(2,1)S(1)}, bf16[2048,256]{0,1:T(8,128)(2,1)S(1)}, u32[]{:S(2)}, u32[]{:S(2)}) %collective-permute-start.70) | collective-permute-done | bytes 1048608 | tf_op jit(solution)/shard_map/ppermute | solution.py:93
  548.4 3.5 fusion.26
  552.0 3.7 collective-permute-start.71
  555.9 3.5 fusion.132
  559.4 16.9 %collective-permute-done.60 = bf16[2048,256]{0,1:T(8,128)(2,1)S(1)} collective-permute-done((bf16[2048,256]{0,1:T(8,128)(2,1)S(1)}, bf16[2048,256]{0,1:T(8,128)(2,1)S(1)}, u32[]{:S(2)}, u32[]{:S(2)}) %collective-permute-start.60) | collective-permute-done | bytes 1048608 | tf_op jit(solution)/shard_map/ppermute | solution.py:93
  576.3 3.5 fusion.30
  579.8 15.8 %collective-permute-start.61 = (bf16[2048,256]{0,1:T(8,128)(2,1)S(1)}, bf16[2048,256]{0,1:T(8,128)(2,1)S(1)}, u32[]{:S(2)}, u32[]{:S(2)}) collective-permute-start(bf16[2048,256]{0,1:T(8,128)(2,1)S(1)} %fusion.30), channel_id=1, source_target_pairs={{0,2},{1,3},{2,4},{3,5},{4,6},{5,7},{6,0},{7,1},{8,14},{9,15},{10,... | collective-permute-start | bytes 3145736 | tf_op jit(solution)/shard_map/ppermute | solution.py:93
  596.4 3.5 fusion.27
  605.9 3.5 fusion.131
  609.4 11.9 %collective-permute-done.61 = bf16[2048,256]{0,1:T(8,128)(2,1)S(1)} collective-permute-done((bf16[2048,256]{0,1:T(8,128)(2,1)S(1)}, bf16[2048,256]{0,1:T(8,128)(2,1)S(1)}, u32[]{:S(2)}, u32[]{:S(2)}) %collective-permute-start.61) | collective-permute-done | bytes 1048608 | tf_op jit(solution)/shard_map/ppermute | solution.py:93
  621.3 3.5 fusion.31
  624.8 14.1 %collective-permute-done.72 = bf16[2048,256]{0,1:T(8,128)(2,1)S(1)} collective-permute-done((bf16[2048,256]{0,1:T(8,128)(2,1)S(1)}, bf16[2048,256]{0,1:T(8,128)(2,1)S(1)}, u32[]{:S(2)}, u32[]{:S(2)}) %collective-permute-start.72) | collective-permute-done | bytes 1048608 | tf_op jit(solution)/shard_map/ppermute | solution.py:93
  638.9 3.5 fusion.28
  (223 shorter events, 134.9 us)
Async XLA Ops:
  3.4 93.8 %collective-permute-start = (bf16[2048,1024]{1,0:T(8,128)(2,1)}, bf16[2048,1024]{1,0:T(8,128)(2,1)}, u32[]{:S(2)}, u32[]{:S(2)}) collective-permute-start(bf16[2048,1024]{1,0:T(8,128)(2,1)} %param.6), channel_id=1, source_target_pairs={{0,1},{1,0},{2,3},{3,2},{4,5},{5,4},{6,7},{7,6},{8,9},{9,8},{10,11... | collective-permute-start | bytes 12582920 | tf_op jit(solution)/shard_map/ppermute | solution.py:83
  6.3 28.1 %collective-permute-start.2 = (bf16[2048,256]{1,0:T(8,128)(2,1)S(1)}, bf16[2048,256]{1,0:T(8,128)(2,1)}, u32[]{:S(2)}, u32[]{:S(2)}) collective-permute-start(bf16[2048,256]{1,0:T(8,128)(2,1)S(1)} %get-tuple-element.70), channel_id=1, source_target_pairs={{0,2},{1,3},{2,4},{3,5},{4,6},{5,7},{6,0},{7,1},{8,14},{9,15},{10,... | collective-permute-start | bytes 3145736 | tf_op jit(solution)/shard_map/ppermute | solution.py:93
  7.9 46.3 %collective-permute-start.1 = (bf16[2048,256]{1,0:T(8,128)(2,1)}, bf16[2048,256]{1,0:T(8,128)(2,1)}, u32[]{:S(2)}, u32[]{:S(2)}) collective-permute-start(bf16[2048,256]{1,0:T(8,128)(2,1)} %get-tuple-element.71), channel_id=1, source_target_pairs={{0,6},{1,7},{2,0},{3,1},{4,2},{5,3},{6,4},{7,5},{8,10},{9,11},{10,... | collective-permute-start | bytes 3145736 | tf_op jit(solution)/shard_map/ppermute | solution.py:93
  11.2 96.9 %collective-permute-start.19 = (bf16[1024,128]{1,0:T(8,128)(2,1)S(1)}, bf16[1024,128]{1,0:T(8,128)(2,1)S(1)}, u32[]{:S(2)}, u32[]{:S(2)}) collective-permute-start(bf16[1024,128]{1,0:T(8,128)(2,1)S(1)} %get-tuple-element.76), channel_id=1, source_target_pairs={{0,8},{8,0},{16,24},{24,16},{1,9},{9,1},{17,25},{25,17},{2,10},{10... | collective-permute-start | bytes 786440 | tf_op jit(solution)/shard_map/ppermute | solution.py:102
  11.2 98.8 %collective-permute-start.20 = (bf16[1024,128]{1,0:T(8,128)(2,1)}, bf16[1024,128]{1,0:T(8,128)(2,1)S(1)}, u32[]{:S(2)}, u32[]{:S(2)}) collective-permute-start(bf16[1024,128]{1,0:T(8,128)(2,1)} %get-tuple-element.75), channel_id=1, source_target_pairs={{0,16},{8,24},{16,0},{24,8},{1,17},{9,25},{17,1},{25,9},{2,18},{10... | collective-permute-start | bytes 786440 | tf_op jit(solution)/shard_map/ppermute | solution.py:102
  34.4 97.2 %collective-permute-start.9 = (bf16[2048,256]{1,0:T(8,128)(2,1)}, bf16[2048,256]{1,0:T(8,128)(2,1)}, u32[]{:S(2)}, u32[]{:S(2)}) collective-permute-start(bf16[2048,256]{1,0:T(8,128)(2,1)} %collective-permute-done.2), channel_id=1, source_target_pairs={{0,2},{1,3},{2,4},{3,5},{4,6},{5,7},{6,0},{7,1},{8,14},{9,15},{10,... | collective-permute-start | bytes 3145736 | tf_op jit(solution)/shard_map/ppermute | solution.py:93
  54.2 77.4 %collective-permute-start.10 = (bf16[2048,256]{1,0:T(8,128)(2,1)}, bf16[2048,256]{1,0:T(8,128)(2,1)}, u32[]{:S(2)}, u32[]{:S(2)}) collective-permute-start(bf16[2048,256]{1,0:T(8,128)(2,1)} %collective-permute-done.1), channel_id=1, source_target_pairs={{0,6},{1,7},{2,0},{3,1},{4,2},{5,3},{6,4},{7,5},{8,10},{9,11},{10,... | collective-permute-start | bytes 3145736 | tf_op jit(solution)/shard_map/ppermute | solution.py:93
  108.1 27.6 %collective-permute-start.3 = (bf16[2048,256]{1,0:T(8,128)(2,1)}, bf16[2048,256]{1,0:T(8,128)(2,1)}, u32[]{:S(2)}, u32[]{:S(2)}) collective-permute-start(bf16[2048,256]{1,0:T(8,128)(2,1)} %convolution_convert_fusion.3), channel_id=1, source_target_pairs={{0,8},{8,0},{16,24},{24,16},{1,9},{9,1},{17,25},{25,17},{2,10},{10... | collective-permute-start | bytes 3145736 | tf_op jit(solution)/shard_map/ppermute | solution.py:102
  131.6 89.0 %collective-permute-start.14 = (bf16[2048,256]{1,0:T(8,128)(2,1)}, bf16[2048,256]{1,0:T(8,128)(2,1)}, u32[]{:S(2)}, u32[]{:S(2)}) collective-permute-start(bf16[2048,256]{1,0:T(8,128)(2,1)} %collective-permute-done.9), channel_id=1, source_target_pairs={{0,2},{1,3},{2,4},{3,5},{4,6},{5,7},{6,0},{7,1},{8,14},{9,15},{10,... | collective-permute-start | bytes 3145736 | tf_op jit(solution)/shard_map/ppermute | solution.py:93
  133.4 65.1 %collective-permute-start.15 = (bf16[2048,256]{1,0:T(8,128)(2,1)}, bf16[2048,256]{1,0:T(8,128)(2,1)}, u32[]{:S(2)}, u32[]{:S(2)}) collective-permute-start(bf16[2048,256]{1,0:T(8,128)(2,1)} %collective-permute-done.10), channel_id=1, source_target_pairs={{0,6},{1,7},{2,0},{3,1},{4,2},{5,3},{6,4},{7,5},{8,10},{9,11},{10,... | collective-permute-start | bytes 3145736 | tf_op jit(solution)/shard_map/ppermute | solution.py:93
  141.9 24.3 %collective-permute-start.4 = (bf16[2048,256]{1,0:T(8,128)(2,1)S(1)}, bf16[2048,256]{1,0:T(8,128)(2,1)S(1)}, u32[]{:S(2)}, u32[]{:S(2)}) collective-permute-start(bf16[2048,256]{1,0:T(8,128)(2,1)S(1)} %fusion.22), channel_id=1, source_target_pairs={{0,16},{8,24},{16,0},{24,8},{1,17},{9,25},{17,1},{25,9},{2,18},{10... | collective-permute-start | bytes 3145736 | tf_op jit(solution)/shard_map/ppermute | solution.py:102
  148.5 19.3 %collective-permute-start.6 = (bf16[2048,256]{1,0:T(8,128)(2,1)}, bf16[2048,256]{1,0:T(8,128)(2,1)}, u32[]{:S(2)}, u32[]{:S(2)}) collective-permute-start(bf16[2048,256]{1,0:T(8,128)(2,1)} %convolution_convert_fusion.2), channel_id=1, source_target_pairs={{0,8},{8,0},{16,24},{24,16},{1,9},{9,1},{17,25},{25,17},{2,10},{10... | collective-permute-start | bytes 3145736 | tf_op jit(solution)/shard_map/ppermute | solution.py:102
  152.4 21.2 %collective-permute-start.11 = (bf16[2048,256]{1,0:T(8,128)(2,1)S(1)}, bf16[2048,256]{1,0:T(8,128)(2,1)}, u32[]{:S(2)}, u32[]{:S(2)}) collective-permute-start(bf16[2048,256]{1,0:T(8,128)(2,1)S(1)} %convolution_convert_fusion.1), channel_id=1, source_target_pairs={{0,8},{8,0},{16,24},{24,16},{1,9},{9,1},{17,25},{25,17},{2,10},{10... | collective-permute-start | bytes 3145736 | tf_op jit(solution)/shard_map/ppermute | solution.py:102
  172.1 26.0 %collective-permute-start.7 = (bf16[2048,256]{1,0:T(8,128)(2,1)S(1)}, bf16[2048,256]{1,0:T(8,128)(2,1)S(1)}, u32[]{:S(2)}, u32[]{:S(2)}) collective-permute-start(bf16[2048,256]{1,0:T(8,128)(2,1)S(1)} %fusion.23), channel_id=1, source_target_pairs={{0,16},{8,24},{16,0},{24,8},{1,17},{9,25},{17,1},{25,9},{2,18},{10... | collective-permute-start | bytes 3145736 | tf_op jit(solution)/shard_map/ppermute | solution.py:102
  178.2 42.0 %collective-permute-start.12 = (bf16[2048,256]{1,0:T(8,128)(2,1)S(1)}, bf16[2048,256]{1,0:T(8,128)(2,1)S(1)}, u32[]{:S(2)}, u32[]{:S(2)}) collective-permute-start(bf16[2048,256]{1,0:T(8,128)(2,1)S(1)} %fusion.24), channel_id=1, source_target_pairs={{0,16},{8,24},{16,0},{24,8},{1,17},{9,25},{17,1},{25,9},{2,18},{10... | collective-permute-start | bytes 3145736 | tf_op jit(solution)/shard_map/ppermute | solution.py:102
  202.7 17.9 %collective-permute-start.16 = (bf16[2048,256]{1,0:T(8,128)(2,1)S(1)}, bf16[2048,256]{1,0:T(8,128)(2,1)S(1)}, u32[]{:S(2)}, u32[]{:S(2)}) collective-permute-start(bf16[2048,256]{1,0:T(8,128)(2,1)S(1)} %convolution_convert_fusion), channel_id=1, source_target_pairs={{0,8},{8,0},{16,24},{24,16},{1,9},{9,1},{17,25},{25,17},{2,10},{10... | collective-permute-start | bytes 3145736 | tf_op jit(solution)/shard_map/ppermute | solution.py:102
  204.6 28.9 %collective-permute-start.24 = (bf16[2048,128]{1,0:T(8,128)(2,1)S(1)}, bf16[2048,128]{1,0:T(8,128)(2,1)}, u32[]{:S(2)}, u32[]{:S(2)}) collective-permute-start(bf16[2048,128]{1,0:T(8,128)(2,1)S(1)} %get-tuple-element.57), channel_id=1, source_target_pairs={{0,2},{1,3},{2,4},{3,5},{4,6},{5,7},{6,0},{7,1},{8,10},{9,11},{10,... | collective-permute-start | bytes 1572872 | tf_op jit(solution)/shard_map/ppermute | solution.py:99
  220.5 39.3 %collective-permute-start.13 = (bf16[2048,256]{1,0:T(8,128)(2,1)S(1)}, bf16[2048,256]{1,0:T(8,128)(2,1)}, u32[]{:S(2)}, u32[]{:S(2)}) collective-permute-start(bf16[2048,256]{1,0:T(8,128)(2,1)S(1)} %get-tuple-element.61), channel_id=1, source_target_pairs={{0,8},{8,0},{16,24},{24,16},{1,9},{9,1},{17,25},{25,17},{2,10},{10... | collective-permute-start | bytes 3145736 | tf_op jit(solution)/shard_map/ppermute | solution.py:102
  225.3 36.8 %collective-permute-start.17 = (bf16[2048,256]{1,0:T(8,128)(2,1)S(1)}, bf16[2048,256]{1,0:T(8,128)(2,1)}, u32[]{:S(2)}, u32[]{:S(2)}) collective-permute-start(bf16[2048,256]{1,0:T(8,128)(2,1)S(1)} %fusion.25), channel_id=1, source_target_pairs={{0,16},{8,24},{16,0},{24,8},{1,17},{9,25},{17,1},{25,9},{2,18},{10... | collective-permute-start | bytes 3145736 | tf_op jit(solution)/shard_map/ppermute | solution.py:102
  230.0 16.2 %collective-permute-start.25 = (bf16[2048,128]{1,0:T(8,128)(2,1)}, bf16[2048,128]{1,0:T(8,128)(2,1)S(1)}, u32[]{:S(2)}, u32[]{:S(2)}) collective-permute-start(bf16[2048,128]{1,0:T(8,128)(2,1)} %get-tuple-element.55), channel_id=1, source_target_pairs={{0,6},{1,7},{2,0},{3,1},{4,2},{5,3},{6,4},{7,5},{8,14},{9,15},{10,... | collective-permute-start | bytes 1572872 | tf_op jit(solution)/shard_map/ppermute | solution.py:99
  233.5 24.2 %collective-permute-start.27 = (bf16[2048,128]{1,0:T(8,128)(2,1)}, bf16[2048,128]{1,0:T(8,128)(2,1)S(1)}, u32[]{:S(2)}, u32[]{:S(2)}) collective-permute-start(bf16[2048,128]{1,0:T(8,128)(2,1)} %collective-permute-done.24), channel_id=1, source_target_pairs={{0,2},{1,3},{2,4},{3,5},{4,6},{5,7},{6,0},{7,1},{8,10},{9,11},{10,... | collective-permute-start | bytes 1572872 | tf_op jit(solution)/shard_map/ppermute | solution.py:99
  246.2 22.7 %collective-permute-start.28 = (bf16[2048,128]{1,0:T(8,128)(2,1)S(1)}, bf16[2048,128]{1,0:T(8,128)(2,1)S(1)}, u32[]{:S(2)}, u32[]{:S(2)}) collective-permute-start(bf16[2048,128]{1,0:T(8,128)(2,1)S(1)} %collective-permute-done.25), channel_id=1, source_target_pairs={{0,6},{1,7},{2,0},{3,1},{4,2},{5,3},{6,4},{7,5},{8,14},{9,15},{10,... | collective-permute-start | bytes 1572872 | tf_op jit(solution)/shard_map/ppermute | solution.py:99
  257.7 22.5 %collective-permute-start.30 = (bf16[2048,128]{1,0:T(8,128)(2,1)S(1)}, bf16[2048,128]{1,0:T(8,128)(2,1)S(1)}, u32[]{:S(2)}, u32[]{:S(2)}) collective-permute-start(bf16[2048,128]{1,0:T(8,128)(2,1)S(1)} %collective-permute-done.27), channel_id=1, source_target_pairs={{0,2},{1,3},{2,4},{3,5},{4,6},{5,7},{6,0},{7,1},{8,10},{9,11},{10,... | collective-permute-start | bytes 1572872 | tf_op jit(solution)/shard_map/ppermute | solution.py:99
  264.6 27.3 %collective-permute-start.18 = (bf16[2048,256]{1,0:T(8,128)(2,1)S(1)}, bf16[2048,256]{1,0:T(8,128)(2,1)S(1)}, u32[]{:S(2)}, u32[]{:S(2)}) collective-permute-start(bf16[2048,256]{1,0:T(8,128)(2,1)S(1)} %get-tuple-element.59), channel_id=1, source_target_pairs={{0,8},{8,0},{16,24},{24,16},{1,9},{9,1},{17,25},{25,17},{2,10},{10... | collective-permute-start | bytes 3145736 | tf_op jit(solution)/shard_map/ppermute | solution.py:102
  268.9 22.1 %collective-permute-start.31 = (bf16[2048,128]{1,0:T(8,128)(2,1)S(1)}, bf16[2048,128]{1,0:T(8,128)(2,1)S(1)}, u32[]{:S(2)}, u32[]{:S(2)}) collective-permute-start(bf16[2048,128]{1,0:T(8,128)(2,1)S(1)} %collective-permute-done.28), channel_id=1, source_target_pairs={{0,6},{1,7},{2,0},{3,1},{4,2},{5,3},{6,4},{7,5},{8,14},{9,15},{10,... | collective-permute-start | bytes 1572872 | tf_op jit(solution)/shard_map/ppermute | solution.py:99
  296.7 14.9 %collective-permute-start.23 = (bf16[1024,256]{1,0:T(8,128)(2,1)S(1)}, bf16[1024,256]{1,0:T(8,128)(2,1)S(1)}, u32[]{:S(2)}, u32[]{:S(2)}) collective-permute-start(bf16[1024,256]{1,0:T(8,128)(2,1)S(1)} %fusion.66), channel_id=1, source_target_pairs={{0,1},{1,0},{2,3},{3,2},{4,5},{5,4},{6,7},{7,6},{8,9},{9,8},{10,11... | collective-permute-start | bytes 1572872 | tf_op jit(solution)/shard_map/ppermute | solution.py:83
  299.5 23.3 %collective-permute-start.26 = (bf16[1024,256]{1,0:T(8,128)(2,1)S(1)}, bf16[1024,256]{1,0:T(8,128)(2,1)S(1)}, u32[]{:S(2)}, u32[]{:S(2)}) collective-permute-start(bf16[1024,256]{1,0:T(8,128)(2,1)S(1)} %fusion.69), channel_id=1, source_target_pairs={{0,1},{1,0},{2,3},{3,2},{4,5},{5,4},{6,7},{7,6},{8,9},{9,8},{10,11... | collective-permute-start | bytes 1572872 | tf_op jit(solution)/shard_map/ppermute | solution.py:83
  301.9 32.2 %collective-permute-start.29 = (bf16[1024,256]{1,0:T(8,128)(2,1)S(1)}, bf16[1024,256]{1,0:T(8,128)(2,1)S(1)}, u32[]{:S(2)}, u32[]{:S(2)}) collective-permute-start(bf16[1024,256]{1,0:T(8,128)(2,1)S(1)} %fusion.72), channel_id=1, source_target_pairs={{0,1},{1,0},{2,3},{3,2},{4,5},{5,4},{6,7},{7,6},{8,9},{9,8},{10,11... | collective-permute-start | bytes 1572872 | tf_op jit(solution)/shard_map/ppermute | solution.py:83
  304.2 40.1 %collective-permute-start.32 = (bf16[1024,256]{1,0:T(8,128)(2,1)S(1)}, bf16[1024,256]{1,0:T(8,128)(2,1)S(1)}, u32[]{:S(2)}, u32[]{:S(2)}) collective-permute-start(bf16[1024,256]{1,0:T(8,128)(2,1)S(1)} %fusion.75), channel_id=1, source_target_pairs={{0,1},{1,0},{2,3},{3,2},{4,5},{5,4},{6,7},{7,6},{8,9},{9,8},{10,11... | collective-permute-start | bytes 1572872 | tf_op jit(solution)/shard_map/ppermute | solution.py:83
  347.3 24.7 %collective-permute-start.37 = (bf16[2,1024,128]{2,1,0:T(8,128)(2,1)S(1)}, bf16[2,1024,128]{2,1,0:T(8,128)(2,1)S(1)}, u32[]{:S(2)}, u32[]{:S(2)}) collective-permute-start(bf16[2,1024,128]{2,1,0:T(8,128)(2,1)S(1)} %get-tuple-element.66), channel_id=1, source_target_pairs={{0,24},{8,16},{16,8},{24,0},{1,25},{9,17},{17,9},{25,1},{2,26},{10... | collective-permute-start | bytes 1572872 | tf_op jit(solution)/shard_map/ppermute | solution.py:102
  352.8 25.1 %collective-permute-start.47 = (bf16[1024,256]{1,0:T(8,128)(2,1)}, bf16[1024,256]{1,0:T(8,128)(2,1)S(1)}, u32[]{:S(2)}, u32[]{:S(2)}) collective-permute-start(bf16[1024,256]{1,0:T(8,128)(2,1)} %get-tuple-element.33), channel_id=1, source_target_pairs={{0,1},{1,0},{2,3},{3,2},{4,5},{5,4},{6,7},{7,6},{8,9},{9,8},{10,11... | collective-permute-start | bytes 1572872 | tf_op jit(solution)/shard_map/ppermute | solution.py:83
  359.1 18.9 %collective-permute-start.34 = (bf16[1024,256]{1,0:T(8,128)(2,1)}, bf16[1024,256]{1,0:T(8,128)(2,1)S(1)}, u32[]{:S(2)}, u32[]{:S(2)}) collective-permute-start(bf16[1024,256]{1,0:T(8,128)(2,1)} %get-tuple-element.36), channel_id=1, source_target_pairs={{0,8},{8,0},{16,24},{24,16},{1,9},{9,1},{17,25},{25,17},{2,10},{10... | collective-permute-start | bytes 1572872 | tf_op jit(solution)/shard_map/ppermute | solution.py:102
  366.4 17.6 %collective-permute-start.36 = (bf16[1024,256]{1,0:T(8,128)(2,1)}, bf16[1024,256]{1,0:T(8,128)(2,1)S(1)}, u32[]{:S(2)}, u32[]{:S(2)}) collective-permute-start(bf16[1024,256]{1,0:T(8,128)(2,1)} %get-tuple-element.39), channel_id=1, source_target_pairs={{0,16},{8,24},{16,0},{24,8},{1,17},{9,25},{17,1},{25,9},{2,18},{10... | collective-permute-start | bytes 1572872 | tf_op jit(solution)/shard_map/ppermute | solution.py:102
  377.1 17.4 %collective-permute-start.38 = (bf16[1024,256]{1,0:T(8,128)(2,1)}, bf16[1024,256]{1,0:T(8,128)(2,1)S(1)}, u32[]{:S(2)}, u32[]{:S(2)}) collective-permute-start(bf16[1024,256]{1,0:T(8,128)(2,1)} %get-tuple-element.42), channel_id=1, source_target_pairs={{0,24},{8,16},{16,8},{24,0},{1,25},{9,17},{17,9},{25,1},{2,26},{10... | collective-permute-start | bytes 1572872 | tf_op jit(solution)/shard_map/ppermute | solution.py:102
  396.1 14.8 %collective-permute-start.48 = (bf16[1024,256]{1,0:T(8,128)(2,1)S(1)}, bf16[1024,256]{1,0:T(8,128)(2,1)S(1)}, u32[]{:S(2)}, u32[]{:S(2)}) collective-permute-start(bf16[1024,256]{1,0:T(8,128)(2,1)S(1)} %collective-permute-done.34), channel_id=1, source_target_pairs={{0,1},{1,0},{2,3},{3,2},{4,5},{5,4},{6,7},{7,6},{8,9},{9,8},{10,11... | collective-permute-start | bytes 1572872 | tf_op jit(solution)/shard_map/ppermute | solution.py:83
  397.6 24.5 %collective-permute-start.49 = (bf16[1024,256]{1,0:T(8,128)(2,1)S(1)}, bf16[1024,256]{1,0:T(8,128)(2,1)S(1)}, u32[]{:S(2)}, u32[]{:S(2)}) collective-permute-start(bf16[1024,256]{1,0:T(8,128)(2,1)S(1)} %collective-permute-done.36), channel_id=1, source_target_pairs={{0,1},{1,0},{2,3},{3,2},{4,5},{5,4},{6,7},{7,6},{8,9},{9,8},{10,11... | collective-permute-start | bytes 1572872 | tf_op jit(solution)/shard_map/ppermute | solution.py:83
  398.9 36.1 %collective-permute-start.39 = (bf16[1024,256]{1,0:T(8,128)(2,1)S(1)}, bf16[1024,256]{1,0:T(8,128)(2,1)S(1)}, u32[]{:S(2)}, u32[]{:S(2)}) collective-permute-start(bf16[1024,256]{1,0:T(8,128)(2,1)S(1)} %convolution_convert_fusion.11), channel_id=1, source_target_pairs={{0,8},{8,0},{16,24},{24,16},{1,9},{9,1},{17,25},{25,17},{2,10},{10... | collective-permute-start | bytes 1572872 | tf_op jit(solution)/shard_map/ppermute | solution.py:102
  399.0 37.4 %collective-permute-start.40 = (bf16[1024,256]{1,0:T(8,128)(2,1)S(1)}, bf16[1024,256]{1,0:T(8,128)(2,1)S(1)}, u32[]{:S(2)}, u32[]{:S(2)}) collective-permute-start(bf16[1024,256]{1,0:T(8,128)(2,1)S(1)} %convolution_convert_fusion.10), channel_id=1, source_target_pairs={{0,8},{8,0},{16,24},{24,16},{1,9},{9,1},{17,25},{25,17},{2,10},{10... | collective-permute-start | bytes 1572872 | tf_op jit(solution)/shard_map/ppermute | solution.py:102
  399.5 33.1 %collective-permute-start.50 = (bf16[1024,256]{1,0:T(8,128)(2,1)S(1)}, bf16[1024,256]{1,0:T(8,128)(2,1)S(1)}, u32[]{:S(2)}, u32[]{:S(2)}) collective-permute-start(bf16[1024,256]{1,0:T(8,128)(2,1)S(1)} %collective-permute-done.38), channel_id=1, source_target_pairs={{0,1},{1,0},{2,3},{3,2},{4,5},{5,4},{6,7},{7,6},{8,9},{9,8},{10,11... | collective-permute-start | bytes 1572872 | tf_op jit(solution)/shard_map/ppermute | solution.py:83
  410.9 28.4 %collective-permute-start.41 = (bf16[1024,256]{1,0:T(8,128)(2,1)S(1)}, bf16[1024,256]{1,0:T(8,128)(2,1)S(1)}, u32[]{:S(2)}, u32[]{:S(2)}) collective-permute-start(bf16[1024,256]{1,0:T(8,128)(2,1)S(1)} %convolution_convert_fusion.9), channel_id=1, source_target_pairs={{0,8},{8,0},{16,24},{24,16},{1,9},{9,1},{17,25},{25,17},{2,10},{10... | collective-permute-start | bytes 1572872 | tf_op jit(solution)/shard_map/ppermute | solution.py:102
  422.1 15.9 %collective-permute-start.42 = (bf16[1024,256]{1,0:T(8,128)(2,1)S(1)}, bf16[1024,256]{1,0:T(8,128)(2,1)S(1)}, u32[]{:S(2)}, u32[]{:S(2)}) collective-permute-start(bf16[1024,256]{1,0:T(8,128)(2,1)S(1)} %convolution_convert_fusion.8), channel_id=1, source_target_pairs={{0,8},{8,0},{16,24},{24,16},{1,9},{9,1},{17,25},{25,17},{2,10},{10... | collective-permute-start | bytes 1572872 | tf_op jit(solution)/shard_map/ppermute | solution.py:102
  433.5 20.9 %collective-permute-start.51 = (bf16[1024,256]{1,0:T(8,128)(2,1)S(1)}, bf16[1024,256]{1,0:T(8,128)(2,1)S(1)}, u32[]{:S(2)}, u32[]{:S(2)}) collective-permute-start(bf16[1024,256]{1,0:T(8,128)(2,1)S(1)} %convolution_convert_fusion.7), channel_id=1, source_target_pairs={{0,8},{8,0},{16,24},{24,16},{1,9},{9,1},{17,25},{25,17},{2,10},{10... | collective-permute-start | bytes 1572872 | tf_op jit(solution)/shard_map/ppermute | solution.py:102
  435.1 20.7 %collective-permute-start.52 = (bf16[1024,256]{1,0:T(8,128)(2,1)S(1)}, bf16[1024,256]{1,0:T(8,128)(2,1)S(1)}, u32[]{:S(2)}, u32[]{:S(2)}) collective-permute-start(bf16[1024,256]{1,0:T(8,128)(2,1)S(1)} %convolution_convert_fusion.6), channel_id=1, source_target_pairs={{0,8},{8,0},{16,24},{24,16},{1,9},{9,1},{17,25},{25,17},{2,10},{10... | collective-permute-start | bytes 1572872 | tf_op jit(solution)/shard_map/ppermute | solution.py:102
  436.4 20.1 %collective-permute-start.53 = (bf16[1024,256]{1,0:T(8,128)(2,1)S(1)}, bf16[1024,256]{1,0:T(8,128)(2,1)S(1)}, u32[]{:S(2)}, u32[]{:S(2)}) collective-permute-start(bf16[1024,256]{1,0:T(8,128)(2,1)S(1)} %convolution_convert_fusion.5), channel_id=1, source_target_pairs={{0,8},{8,0},{16,24},{24,16},{1,9},{9,1},{17,25},{25,17},{2,10},{10... | collective-permute-start | bytes 1572872 | tf_op jit(solution)/shard_map/ppermute | solution.py:102
  439.3 14.8 %collective-permute-start.43 = (bf16[1024,256]{1,0:T(8,128)(2,1)S(1)}, bf16[1024,256]{1,0:T(8,128)(2,1)S(1)}, u32[]{:S(2)}, u32[]{:S(2)}) collective-permute-start(bf16[1024,256]{1,0:T(8,128)(2,1)S(1)} %fusion.61), channel_id=1, source_target_pairs={{0,16},{8,24},{16,0},{24,8},{1,17},{9,25},{17,1},{25,9},{2,18},{10... | collective-permute-start | bytes 1572872 | tf_op jit(solution)/shard_map/ppermute | solution.py:102
  441.5 24.0 %collective-permute-start.55 = (bf16[1024,256]{1,0:T(8,128)(2,1)S(1)}, bf16[1024,256]{1,0:T(8,128)(2,1)S(1)}, u32[]{:S(2)}, u32[]{:S(2)}) collective-permute-start(bf16[1024,256]{1,0:T(8,128)(2,1)S(1)} %fusion.65), channel_id=1, source_target_pairs={{0,16},{8,24},{16,0},{24,8},{1,17},{9,25},{17,1},{25,9},{2,18},{10... | collective-permute-start | bytes 1572872 | tf_op jit(solution)/shard_map/ppermute | solution.py:102
  454.3 48.1 %collective-permute-start.68 = (bf16[1024,256]{1,0:T(8,128)(2,1)S(1)}, bf16[1024,256]{1,0:T(8,128)(2,1)S(1)}, u32[]{:S(2)}, u32[]{:S(2)}) collective-permute-start(bf16[1024,256]{1,0:T(8,128)(2,1)S(1)} %add_convert_fusion.11), channel_id=1, source_target_pairs={{0,8},{8,0},{16,24},{24,16},{1,9},{9,1},{17,25},{25,17},{2,10},{10... | collective-permute-start | bytes 1572872 | tf_op jit(solution)/shard_map/ppermute | solution.py:102
  454.4 22.2 %collective-permute-start.44 = (bf16[1024,256]{1,0:T(8,128)(2,1)S(1)}, bf16[1024,256]{1,0:T(8,128)(2,1)S(1)}, u32[]{:S(2)}, u32[]{:S(2)}) collective-permute-start(bf16[1024,256]{1,0:T(8,128)(2,1)S(1)} %fusion.60), channel_id=1, source_target_pairs={{0,16},{8,24},{16,0},{24,8},{1,17},{9,25},{17,1},{25,9},{2,18},{10... | collective-permute-start | bytes 1572872 | tf_op jit(solution)/shard_map/ppermute | solution.py:102
  465.5 33.3 %collective-permute-start.69 = (bf16[1024,256]{1,0:T(8,128)(2,1)S(1)}, bf16[1024,256]{1,0:T(8,128)(2,1)S(1)}, u32[]{:S(2)}, u32[]{:S(2)}) collective-permute-start(bf16[1024,256]{1,0:T(8,128)(2,1)S(1)} %add_convert_fusion.7), channel_id=1, source_target_pairs={{0,8},{8,0},{16,24},{24,16},{1,9},{9,1},{17,25},{25,17},{2,10},{10... | collective-permute-start | bytes 1572872 | tf_op jit(solution)/shard_map/ppermute | solution.py:102
  465.6 22.3 %collective-permute-start.56 = (bf16[1024,256]{1,0:T(8,128)(2,1)S(1)}, bf16[1024,256]{1,0:T(8,128)(2,1)S(1)}, u32[]{:S(2)}, u32[]{:S(2)}) collective-permute-start(bf16[1024,256]{1,0:T(8,128)(2,1)S(1)} %fusion.64), channel_id=1, source_target_pairs={{0,16},{8,24},{16,0},{24,8},{1,17},{9,25},{17,1},{25,9},{2,18},{10... | collective-permute-start | bytes 1572872 | tf_op jit(solution)/shard_map/ppermute | solution.py:102
  476.8 57.7 %collective-permute-start.66 = (bf16[1024,256]{1,0:T(8,128)(2,1)S(1)}, bf16[1024,256]{1,0:T(8,128)(2,1)S(1)}, u32[]{:S(2)}, u32[]{:S(2)}) collective-permute-start(bf16[1024,256]{1,0:T(8,128)(2,1)S(1)} %add_convert_fusion.10), channel_id=1, source_target_pairs={{0,8},{8,0},{16,24},{24,16},{1,9},{9,1},{17,25},{25,17},{2,10},{10... | collective-permute-start | bytes 1572872 | tf_op jit(solution)/shard_map/ppermute | solution.py:102
  476.9 21.3 %collective-permute-start.45 = (bf16[1024,256]{1,0:T(8,128)(2,1)S(1)}, bf16[1024,256]{1,0:T(8,128)(2,1)S(1)}, u32[]{:S(2)}, u32[]{:S(2)}) collective-permute-start(bf16[1024,256]{1,0:T(8,128)(2,1)S(1)} %fusion.59), channel_id=1, source_target_pairs={{0,16},{8,24},{16,0},{24,8},{1,17},{9,25},{17,1},{25,9},{2,18},{10... | collective-permute-start | bytes 1572872 | tf_op jit(solution)/shard_map/ppermute | solution.py:102
  487.9 42.5 %collective-permute-start.59 = (bf16[2048,256]{0,1:T(8,128)(2,1)S(1)}, bf16[2048,256]{0,1:T(8,128)(2,1)S(1)}, u32[]{:S(2)}, u32[]{:S(2)}) collective-permute-start(bf16[2048,256]{0,1:T(8,128)(2,1)S(1)} %fusion.32), channel_id=1, source_target_pairs={{0,2},{1,3},{2,4},{3,5},{4,6},{5,7},{6,0},{7,1},{8,14},{9,15},{10,... | collective-permute-start | bytes 3145736 | tf_op jit(solution)/shard_map/ppermute | solution.py:93
  498.9 96.8 %collective-permute-start.64 = (bf16[1024,256]{1,0:T(8,128)(2,1)S(1)}, bf16[1024,256]{1,0:T(8,128)(2,1)S(1)}, u32[]{:S(2)}, u32[]{:S(2)}) collective-permute-start(bf16[1024,256]{1,0:T(8,128)(2,1)S(1)} %add_convert_fusion.9), channel_id=1, source_target_pairs={{0,8},{8,0},{16,24},{24,16},{1,9},{9,1},{17,25},{25,17},{2,10},{10... | collective-permute-start | bytes 1572872 | tf_op jit(solution)/shard_map/ppermute | solution.py:102
  502.4 24.4 %collective-permute-start.67 = (bf16[1024,256]{1,0:T(8,128)(2,1)S(1)}, bf16[1024,256]{1,0:T(8,128)(2,1)S(1)}, u32[]{:S(2)}, u32[]{:S(2)}) collective-permute-start(bf16[1024,256]{1,0:T(8,128)(2,1)S(1)} %add_convert_fusion.6), channel_id=1, source_target_pairs={{0,8},{8,0},{16,24},{24,16},{1,9},{9,1},{17,25},{25,17},{2,10},{10... | collective-permute-start | bytes 1572872 | tf_op jit(solution)/shard_map/ppermute | solution.py:102
  523.3 25.0 %collective-permute-start.70 = (bf16[2048,256]{0,1:T(8,128)(2,1)S(1)}, bf16[2048,256]{0,1:T(8,128)(2,1)S(1)}, u32[]{:S(2)}, u32[]{:S(2)}) collective-permute-start(bf16[2048,256]{0,1:T(8,128)(2,1)S(1)} %fusion.33), channel_id=1, source_target_pairs={{0,6},{1,7},{2,0},{3,1},{4,2},{5,3},{6,4},{7,5},{8,10},{9,11},{10,... | collective-permute-start | bytes 3145736 | tf_op jit(solution)/shard_map/ppermute | solution.py:93
  526.8 29.0 %collective-permute-start.65 = (bf16[1024,256]{1,0:T(8,128)(2,1)S(1)}, bf16[1024,256]{1,0:T(8,128)(2,1)S(1)}, u32[]{:S(2)}, u32[]{:S(2)}) collective-permute-start(bf16[1024,256]{1,0:T(8,128)(2,1)S(1)} %add_convert_fusion.5), channel_id=1, source_target_pairs={{0,8},{8,0},{16,24},{24,16},{1,9},{9,1},{17,25},{25,17},{2,10},{10... | collective-permute-start | bytes 1572872 | tf_op jit(solution)/shard_map/ppermute | solution.py:102
  530.4 21.6 %collective-permute-start.58 = (bf16[1024,256]{1,0:T(8,128)(2,1)S(1)}, bf16[1024,256]{1,0:T(8,128)(2,1)S(1)}, u32[]{:S(2)}, u32[]{:S(2)}) collective-permute-start(bf16[1024,256]{1,0:T(8,128)(2,1)S(1)} %fusion.62), channel_id=1, source_target_pairs={{0,16},{8,24},{16,0},{24,8},{1,17},{9,25},{17,1},{25,9},{2,18},{10... | collective-permute-start | bytes 1572872 | tf_op jit(solution)/shard_map/ppermute | solution.py:102
  534.5 90.4 %collective-permute-start.62 = (bf16[1024,256]{1,0:T(8,128)(2,1)S(1)}, bf16[1024,256]{1,0:T(8,128)(2,1)S(1)}, u32[]{:S(2)}, u32[]{:S(2)}) collective-permute-start(bf16[1024,256]{1,0:T(8,128)(2,1)S(1)} %add_convert_fusion.8), channel_id=1, source_target_pairs={{0,8},{8,0},{16,24},{24,16},{1,9},{9,1},{17,25},{25,17},{2,10},{10... | collective-permute-start | bytes 1572872 | tf_op jit(solution)/shard_map/ppermute | solution.py:102
  548.3 28.0 %collective-permute-start.60 = (bf16[2048,256]{0,1:T(8,128)(2,1)S(1)}, bf16[2048,256]{0,1:T(8,128)(2,1)S(1)}, u32[]{:S(2)}, u32[]{:S(2)}) collective-permute-start(bf16[2048,256]{0,1:T(8,128)(2,1)S(1)} %fusion.29), channel_id=1, source_target_pairs={{0,2},{1,3},{2,4},{3,5},{4,6},{5,7},{6,0},{7,1},{8,14},{9,15},{10,... | collective-permute-start | bytes 3145736 | tf_op jit(solution)/shard_map/ppermute | solution.py:93
  552.0 44.5 %collective-permute-start.71 = (bf16[2048,256]{0,1:T(8,128)(2,1)S(1)}, bf16[2048,256]{0,1:T(8,128)(2,1)S(1)}, u32[]{:S(2)}, u32[]{:S(2)}) collective-permute-start(bf16[2048,256]{0,1:T(8,128)(2,1)S(1)} %fusion.26), channel_id=1, source_target_pairs={{0,6},{1,7},{2,0},{3,1},{4,2},{5,3},{6,4},{7,5},{8,10},{9,11},{10,... | collective-permute-start | bytes 3145736 | tf_op jit(solution)/shard_map/ppermute | solution.py:93
  555.8 50.1 %collective-permute-start.63 = (bf16[1024,256]{1,0:T(8,128)(2,1)S(1)}, bf16[1024,256]{1,0:T(8,128)(2,1)S(1)}, u32[]{:S(2)}, u32[]{:S(2)}) collective-permute-start(bf16[1024,256]{1,0:T(8,128)(2,1)S(1)} %add_convert_fusion.4), channel_id=1, source_target_pairs={{0,8},{8,0},{16,24},{24,16},{1,9},{9,1},{17,25},{25,17},{2,10},{10... | collective-permute-start | bytes 1572872 | tf_op jit(solution)/shard_map/ppermute | solution.py:102
  579.8 41.4 %collective-permute-start.61 = (bf16[2048,256]{0,1:T(8,128)(2,1)S(1)}, bf16[2048,256]{0,1:T(8,128)(2,1)S(1)}, u32[]{:S(2)}, u32[]{:S(2)}) collective-permute-start(bf16[2048,256]{0,1:T(8,128)(2,1)S(1)} %fusion.30), channel_id=1, source_target_pairs={{0,2},{1,3},{2,4},{3,5},{4,6},{5,7},{6,0},{7,1},{8,14},{9,15},{10,... | collective-permute-start | bytes 3145736 | tf_op jit(solution)/shard_map/ppermute | solution.py:93
  600.0 39.0 %collective-permute-start.72 = (bf16[2048,256]{0,1:T(8,128)(2,1)S(1)}, bf16[2048,256]{0,1:T(8,128)(2,1)S(1)}, u32[]{:S(2)}, u32[]{:S(2)}) collective-permute-start(bf16[2048,256]{0,1:T(8,128)(2,1)S(1)} %fusion.27), channel_id=1, source_target_pairs={{0,6},{1,7},{2,0},{3,1},{4,2},{5,3},{6,4},{7,5},{8,10},{9,11},{10,... | collective-permute-start | bytes 3145736 | tf_op jit(solution)/shard_map/ppermute | solution.py:93
  (25 other events, 250.9 us)
